TPU v7x, 32 devices: a whole 2x2x4 slice. The times are simulated.
32 devices in a mesh: blk: 8 (over z, y), head: 4 (over x, core).
Axes of the slice: x: 2, y: 2, z: 4, core: 2. Of those that a mesh axis runs over, the one named last changes fastest.
Arguments:
- inputs: bfloat16 [4096, 704], P('blk'), may hold values from -6 to 6
- out_queries: bfloat16 [8192, 1026], P('blk'), may hold values from -6 to 6
- clip_lengths: int32 [6], replicated, may hold values from 1 to 7767, as said below
- labels: int32 [8192], P('blk'), may hold values from 0 to 703
- modality: int32 [8192], P('blk'), may hold values from 0 to 2
- labeled: int32 [8192], P('blk'), may hold values from 0 to 1
- head_params: float32 [4751360], P(('head', 'blk')), may hold values from -4 to 4
- head_first: float32 [4751360], P(('head', 'blk')), may hold values from -1 to 1
- head_second: float32 [4751360], P(('head', 'blk')), may hold values from 0 to 1
- common_params: float32 [928768], P('blk'), may hold values from -4 to 4
- common_first: float32 [928768], P('blk'), may hold values from -1 to 1
- common_second: float32 [928768], P('blk'), may hold values from 0 to 1
Outputs:
- head_new: float32 [4751360], P(('head', 'blk'))
- head_first_new: float32 [4751360], P(('head', 'blk'))
- head_second_new: float32 [4751360], P(('head', 'blk'))
- head_copy: bfloat16 [4751360], P(('head', 'blk'))
- common_new: float32 [928768], P('blk')
- common_first_new: float32 [928768], P('blk')
- common_second_new: float32 [928768], P('blk')
- common_copy: bfloat16 [928768], P('blk')
- loss_sums: float32 [3], replicated
- label_counts: float32 [3], replicated
- clip_norm: float32 [], replicated
Inputs may be any that keep to these rules, and one draw needn't show every extreme that they name: `clip_lengths`: 6 lengths summing to 8192; one clip, at a place drawn from the seed, holds exactly the largest length and runs from the rows of the first index of blk to those of the last; the others hold together (5) * (85) rows, each fewer than 170.
All inputs are finite; a program needn't handle non-finite values.
Results may differ from a plain program's by a relative error of at most 0.017.
Values may be sent and summed in bfloat16 or wider, within the bound.
A program may use at most 192 MiB of HBM per device.

v0:
```python
import math

import jax
import jax.numpy as jnp
from jax import lax
from jax.sharding import PartitionSpec as P

D = 512
HEADS = 8
HD = 64
FF = 2048
DI = 704
DQ = 1026
C = 704
LAT = 784
MODES = 3
STEP = 10


highest = lax.Precision.HIGHEST
norm_eps = 1e-05
learn_rate = 0.1
beta_one = 0.9
beta_two = 0.999
adam_eps = 1e-08
weight_decay = 0.01
clip_limit = 0.05
big_negative = -1e30


def joined(value, axis, combine):
    everything = jax.tree.map(lambda part: lax.all_gather(part, axis), value)
    initial = jax.tree.map(lambda part: part[0], everything)

    def hop(k, so_far):
        return combine(so_far, jax.tree.map(lambda part: part[k], everything))

    return lax.fori_loop(1, lax.axis_size(axis), hop, initial)


def layer_norm(x, gain):
    centre = x - jnp.mean(x, -1, keepdims=True)
    return centre * lax.rsqrt(jnp.mean(centre * centre, -1, keepdims=True) + norm_eps) * gain


def norm_pullback(x, gain, grad):
    unused, pull = jax.vjp(layer_norm, x, gain)
    return pull(grad)


def product(a, b):
    return jnp.dot(a, b, preferred_element_type=jnp.float32)


def inner(a, b):
    return lax.dot_general(a, b, (((0,), (0,)), ((), ())), preferred_element_type=jnp.float32)


def against(a, b):
    return lax.dot_general(a, b, (((1,), (1,)), ((), ())), preferred_element_type=jnp.float32)


def slice_rows(array, first, amount):
    return lax.dynamic_slice_in_dim(array, first, amount, 0)


def clip_index(lengths, first, amount):
    places = first + jnp.arange(amount, dtype=jnp.int32)
    finish = jnp.cumsum(lengths)
    clip_id = jnp.sum((places[:, None] >= finish[None, :]).astype(jnp.int32), 1)
    begins = finish - lengths
    clip_numbers = jnp.arange(lengths.shape[0], dtype=jnp.int32)
    opening = jnp.sum(jnp.where(clip_id[:, None] == clip_numbers[None, :], begins[None, :], 0), 1)
    return (clip_id, places - opening)


def head_parts(flat, n_head):
    width = HEADS // n_head * HD
    hidden = FF // n_head
    classes = C // n_head
    shapes = (
        (D, width),
        (DI, 2 * width),
        (width, D),
        (D, 3 * width),
        (width, D),
        (D, hidden),
        (hidden, D),
        (D, classes),
    )
    pieces = []
    border = 0
    for shape in shapes:
        amount = shape[0] * shape[1]
        pieces.append(flat[border : border + amount].reshape(shape))
        border += amount
    return pieces


def common_parts(flat):
    border = DQ * D
    query_table = flat[:border].reshape(DQ, D)
    latent_table = flat[border : border + LAT * D].reshape(LAT, D)
    border += LAT * D
    norm_gains = flat[border : border + 4 * D].reshape(4, D)
    return (query_table, latent_table, norm_gains)


def scaled_scores(query, keys):
    return jnp.einsum("qhd,khd->hqk", query, keys, preferred_element_type=jnp.float32) * HD ** (
        -0.5
    )


def attend_local(query, keys, values):
    scores = scaled_scores(query, keys)
    top = jnp.max(scores, -1)
    probs = jnp.exp(scores - top[..., None])
    total = jnp.sum(probs, -1)
    summed = jnp.einsum("hqk,khd->qhd", probs, values.astype(jnp.float32), precision=highest)
    return (summed / total.T[..., None], top + jnp.log(total))


def block_grads(query, keys, values, dout, row_lse, delta, visible):
    scores = scaled_scores(query, keys)
    probs = jnp.where(visible[None], jnp.exp(scores - row_lse[..., None]), 0.0)
    dprob = jnp.einsum("qhd,khd->hqk", dout, values, preferred_element_type=jnp.float32)
    dscore = jnp.where(visible[None], probs * (dprob - delta[..., None]), 0.0).astype(jnp.bfloat16)
    grad_q = jnp.einsum("hqk,khd->qhd", dscore, keys, preferred_element_type=jnp.float32) * HD ** (
        -0.5
    )
    grad_k = jnp.einsum("hqk,qhd->khd", dscore, query, preferred_element_type=jnp.float32) * HD ** (
        -0.5
    )
    grad_v = jnp.einsum("hqk,qhd->khd", probs, dout.astype(jnp.float32), precision=highest)
    return (grad_q, grad_k, grad_v)


def fold_keys(query, query_clip, lengths):

    def fold_piece(carry, piece, start):
        keys, values = piece
        amount = keys.shape[0]
        step_rows = math.gcd(amount, 1024)
        key_clip = clip_index(lengths, start, amount)[0]

        def one_block(state, index):
            top, total, accum = state
            first = index * step_rows
            visible = query_clip[:, None] == slice_rows(key_clip, first, step_rows)[None, :]
            scores = jnp.where(
                visible[None],
                scaled_scores(query, slice_rows(keys, first, step_rows)),
                big_negative,
            )
            new_top = jnp.maximum(top, jnp.max(scores, -1))
            shrink = jnp.exp(top - new_top)
            probs = jnp.where(visible[None], jnp.exp(scores - new_top[..., None]), 0.0)
            total = total * shrink + jnp.sum(probs, -1)
            block_values = slice_rows(values, first, step_rows).astype(jnp.float32)
            accum = accum * shrink[..., None] + jnp.einsum(
                "hqk,khd->hqd", probs, block_values, precision=highest
            )
            return ((new_top, total, accum), None)

        carry, unused = lax.scan(one_block, carry, jnp.arange(amount // step_rows))
        return carry

    return fold_piece


def combine_stats(first, second):
    top = jnp.maximum(first[0], second[0])
    return (
        top,
        first[1] * jnp.exp(first[0] - top) + second[1] * jnp.exp(second[0] - top),
        first[2] + second[2],
    )


def adam_step(weight, first, second, grad):
    first = beta_one * first + (1 - beta_one) * grad
    second = beta_two * second + (1 - beta_two) * grad * grad
    fixed_first = first / (1 - beta_one**STEP)
    fixed_second = second / (1 - beta_two**STEP)
    weight = weight - learn_rate * (
        fixed_first / (jnp.sqrt(fixed_second) + adam_eps) + weight_decay * weight
    )
    return (weight, first, second, weight.astype(jnp.bfloat16))


def per_device(
    inputs,
    out_queries,
    clip_lengths,
    labels,
    modality,
    labeled,
    head_params,
    head_first,
    head_second,
    common_params,
    common_first,
    common_second,
):
    n_head = lax.axis_size("head")
    head_rank = lax.axis_index("head")
    blk_rank = lax.axis_index("blk")
    local_rows = labels.shape[0]
    heads_here = HEADS // n_head
    width = heads_here * HD

    def split_heads(x):
        return x.reshape(x.shape[0], heads_here, HD)

    def over_heads(x):
        return lax.psum(x.astype(jnp.bfloat16), "head").astype(jnp.float32)

    head_flat, common_flat = (
        lax.all_gather(head_params.astype(jnp.bfloat16), "blk", axis=0, tiled=True),
        lax.all_gather(common_params.astype(jnp.bfloat16), "blk", axis=0, tiled=True),
    )
    (
        enc_query,
        enc_keyval,
        enc_output,
        self_project,
        self_output,
        hidden_in,
        hidden_out,
        class_table,
    ) = head_parts(head_flat, n_head)
    query_table, latent_table, norm_gains = common_parts(common_flat)
    norm_gains = norm_gains.astype(jnp.float32)
    clip_id, offset = clip_index(clip_lengths, blk_rank * local_rows, local_rows)
    latent_rows = offset % LAT
    z_zero = latent_table[latent_rows].astype(jnp.float32)
    h_zero = layer_norm(z_zero, norm_gains[0]).astype(jnp.bfloat16)
    x_norm = layer_norm(inputs.astype(jnp.float32), 1.0).astype(jnp.bfloat16)
    query_enc = product(h_zero, enc_query).astype(jnp.bfloat16)
    keyval_enc = product(x_norm, enc_keyval).astype(jnp.bfloat16)
    keys_enc = split_heads(keyval_enc[:, :width])
    values_enc = split_heads(keyval_enc[:, width:])
    out_enc, lse_enc = attend_local(split_heads(query_enc), keys_enc, values_enc)
    out_enc_low = out_enc.reshape(local_rows, width).astype(jnp.bfloat16)
    z_one = z_zero + over_heads(product(out_enc_low, enc_output))
    h_one = layer_norm(z_one, norm_gains[1]).astype(jnp.bfloat16)
    projected = product(h_one, self_project).astype(jnp.bfloat16)
    query_self = split_heads(projected[:, :width])
    keys_self = split_heads(projected[:, width : 2 * width])
    values_self = split_heads(projected[:, 2 * width :])
    start_state = (
        jnp.full((heads_here, local_rows), big_negative, jnp.float32),
        jnp.zeros((heads_here, local_rows), jnp.float32),
        jnp.zeros((heads_here, local_rows, HD), jnp.float32),
    )
    folding = fold_keys(query_self, clip_id, clip_lengths)
    state = folding(
        start_state,
        (
            lax.all_gather(keys_self, "blk", axis=0, tiled=True),
            lax.all_gather(values_self, "blk", axis=0, tiled=True),
        ),
        jnp.int32(0),
    )
    top, total, accum = state
    out_self = jnp.transpose(accum / total[..., None], (1, 0, 2))
    lse_self = top + jnp.log(total)
    out_self_low = out_self.reshape(local_rows, width).astype(jnp.bfloat16)
    z_two = z_one + over_heads(product(out_self_low, self_output))
    h_two = layer_norm(z_two, norm_gains[2]).astype(jnp.bfloat16)
    pre_act = product(h_two, hidden_in)
    activ = jax.nn.gelu(pre_act).astype(jnp.bfloat16)
    z_three = z_two + over_heads(product(activ, hidden_out))
    decoded = layer_norm(z_three, norm_gains[3]) + product(out_queries, query_table)
    decoded_low = decoded.astype(jnp.bfloat16)
    logits = product(decoded_low, class_table)
    class_here = class_table.shape[1]
    class_ids = head_rank * class_here + jnp.arange(class_here, dtype=jnp.int32)
    is_target = labels[:, None] == class_ids[None, :]
    local_top = jnp.max(logits, -1)
    local_sum = jnp.sum(jnp.exp(logits - local_top[:, None]), -1)
    local_target = jnp.sum(jnp.where(is_target, logits, 0.0), -1)
    row_top, row_sum, target = joined((local_top, local_sum, local_target), "head", combine_stats)
    row_lse = row_top + jnp.log(row_sum)
    member = (
        (modality[:, None] == jnp.arange(MODES, dtype=jnp.int32)[None, :]) & (labeled[:, None] == 1)
    ).astype(jnp.float32)
    loss_sums, label_counts = lax.psum(
        (jnp.sum((row_lse - target)[:, None] * member, 0), jnp.sum(member, 0)), "blk"
    )
    row_weight = jnp.sum(member / jnp.maximum(label_counts, 1.0)[None, :], 1)
    dlogits = (
        row_weight[:, None] * (jnp.exp(logits - row_lse[:, None]) - is_target.astype(jnp.float32))
    ).astype(jnp.bfloat16)
    class_grad = inner(decoded_low, dlogits)
    d_decoded = over_heads(against(dlogits, class_table))
    query_grad = inner(out_queries, d_decoded.astype(jnp.bfloat16))
    d_three, gain_three = norm_pullback(z_three, norm_gains[3], d_decoded)
    d_branch = d_three.astype(jnp.bfloat16)
    out_grad = inner(activ, d_branch)
    unused, gelu_pull = jax.vjp(jax.nn.gelu, pre_act)
    d_pre = gelu_pull(against(d_branch, hidden_out))[0].astype(jnp.bfloat16)
    in_grad = inner(h_two, d_pre)
    d_middle, gain_two = norm_pullback(z_two, norm_gains[2], over_heads(against(d_pre, hidden_in)))
    d_two = d_three + d_middle
    d_branch = d_two.astype(jnp.bfloat16)
    self_out_grad = inner(out_self_low, d_branch)
    dout_self = against(d_branch, self_output).astype(jnp.bfloat16)
    dout_heads = split_heads(dout_self)
    delta_self = jnp.einsum("qhd,qhd->hq", dout_heads.astype(jnp.float32), out_self)
    keys_all, values_all = (
        lax.all_gather(keys_self, "blk", axis=0, tiled=True),
        lax.all_gather(values_self, "blk", axis=0, tiled=True),
    )
    amount_all = keys_all.shape[0]
    step_rows = math.gcd(amount_all, 1024)

    def key_block(acc, index):
        first = index * step_rows
        block_clip = clip_index(clip_lengths, first, step_rows)[0]
        visible = clip_id[:, None] == block_clip[None, :]
        grad_q, grad_k, grad_v = block_grads(
            query_self,
            slice_rows(keys_all, first, step_rows),
            slice_rows(values_all, first, step_rows),
            dout_heads,
            lse_self,
            delta_self,
            visible,
        )
        return (acc + grad_q, (grad_k, grad_v))

    zero_rows = jnp.zeros((local_rows, heads_here, HD), jnp.float32)
    grad_query, key_parts = lax.scan(key_block, zero_rows, jnp.arange(amount_all // step_rows))
    grad_keys, grad_values = (
        lax.psum_scatter(
            key_parts[0].reshape(amount_all, width).astype(jnp.bfloat16),
            "blk",
            scatter_dimension=0,
            tiled=True,
        ).astype(jnp.float32),
        lax.psum_scatter(
            key_parts[1].reshape(amount_all, width).astype(jnp.bfloat16),
            "blk",
            scatter_dimension=0,
            tiled=True,
        ).astype(jnp.float32),
    )
    d_project = jnp.concatenate(
        [
            grad_query.reshape(local_rows, width).astype(jnp.bfloat16),
            grad_keys.astype(jnp.bfloat16),
            grad_values.astype(jnp.bfloat16),
        ],
        1,
    )
    project_grad = inner(h_one, d_project)
    d_middle, gain_one = norm_pullback(
        z_one, norm_gains[1], over_heads(against(d_project, self_project))
    )
    d_one = d_two + d_middle
    d_branch = d_one.astype(jnp.bfloat16)
    enc_out_grad = inner(out_enc_low, d_branch)
    dout_enc = split_heads(against(d_branch, enc_output).astype(jnp.bfloat16))
    delta_enc = jnp.einsum("qhd,qhd->hq", dout_enc.astype(jnp.float32), out_enc)
    every = jnp.ones((local_rows, inputs.shape[0]), bool)
    grad_q, grad_k, grad_v = block_grads(
        split_heads(query_enc), keys_enc, values_enc, dout_enc, lse_enc, delta_enc, every
    )
    d_query_enc = grad_q.reshape(local_rows, width).astype(jnp.bfloat16)
    d_keyval_enc = jnp.concatenate(
        [
            grad_k.reshape(-1, width).astype(jnp.bfloat16),
            grad_v.reshape(-1, width).astype(jnp.bfloat16),
        ],
        1,
    )
    enc_query_grad = inner(h_zero, d_query_enc)
    enc_keyval_grad = inner(x_norm, d_keyval_enc)
    d_hzero = over_heads(against(d_query_enc, enc_query))
    d_middle, gain_zero = norm_pullback(z_zero, norm_gains[0], d_hzero)
    d_zero = d_one + d_middle
    latent_grad = jax.ops.segment_sum(d_zero, latent_rows, LAT)
    head_grad = jnp.concatenate(
        [
            g.reshape(-1)
            for g in (
                enc_query_grad,
                enc_keyval_grad,
                enc_out_grad,
                project_grad,
                self_out_grad,
                in_grad,
                out_grad,
                class_grad,
            )
        ]
    )
    common_grad = jnp.concatenate(
        [
            query_grad.reshape(-1),
            latent_grad.reshape(-1),
            jnp.stack([gain_zero, gain_one, gain_two, gain_three]).reshape(-1),
        ]
    )
    head_share, common_share = (
        lax.psum_scatter(
            head_grad.astype(jnp.bfloat16), "blk", scatter_dimension=0, tiled=True
        ).astype(jnp.float32),
        lax.psum_scatter(
            common_grad.astype(jnp.bfloat16), "blk", scatter_dimension=0, tiled=True
        ).astype(jnp.float32),
    )
    squares = jnp.sum(head_share * head_share) + jnp.sum(common_share * common_share) / n_head
    clip_norm = jnp.sqrt(lax.psum(squares, ("blk", "head")))
    factor = jnp.minimum(1.0, clip_limit / clip_norm)
    head_out = adam_step(head_params, head_first, head_second, head_share * factor)
    common_out = adam_step(common_params, common_first, common_second, common_share * factor)
    return head_out + common_out + (loss_sums, label_counts, clip_norm)


def solution(mesh):
    placed = (
        P("blk", None),
        P("blk", None),
        P(),
        P("blk"),
        P("blk"),
        P("blk"),
        P(("head", "blk")),
        P(("head", "blk")),
        P(("head", "blk")),
        P("blk"),
        P("blk"),
        P("blk"),
    )
    return jax.shard_map(
        per_device,
        mesh=mesh,
        in_specs=placed,
        out_specs=(
            P(("head", "blk")),
            P(("head", "blk")),
            P(("head", "blk")),
            P(("head", "blk")),
            P("blk"),
            P("blk"),
            P("blk"),
            P("blk"),
            P(),
            P(),
            P(),
        ),
        check_vma=False,
    )
```

profile of v0, /device:TPU:0, one launch (start us, length us, event | category | flops | bytes accessed | tf_op | source)
XLA Modules:
  0.0 1312.5 jit_solution(11768717461921295786)
XLA Ops:
  13.3 67.6 %all-gather.15.cloned.1.call-done = bf16[8,1,116096]{2,1,0:T(2,128)(2,1)} async-done(((bf16[1,1,116096]{2,1,0:T(2,128)(2,1)}), bf16[8,1,116096]{2,1,0:T(2,128)(2,1)}) %all-gather.15.cloned.1.call-update) | async-done | bytes 1857552 | tf_op jit(solution)/shard_map/all_gather | solution.py:221
  80.9 40.7 %reduce.2 = bf16[8,116096]{1,0:T(8,128)(2,1)} reduce(bf16[8,1,116096]{2,1,0:T(2,128)(2,1)} %all-gather.15.cloned.1.call-done, bf16[]{:T(256)} %constant.226), dimensions={1}, to_apply=%all-gather.3.reduce_sub_computation | reduce | bytes 3715074 | tf_op jit(solution)/shard_map/all_gather | solution.py:221
  121.6 5.5 reshape.556
  129.7 5.7 gather_fusion
  153.5 33.7 %all-reduce.12.cloned.1.call-done = bf16[1024,512]{1,0:T(8,128)(2,1)} async-done(((bf16[1024,512]{1,0:T(8,128)(2,1)}), bf16[1024,512]{1,0:T(8,128)(2,1)}) %all-reduce.12.cloned.1.call-update) | async-done | bytes 1048592 | tf_op jit(solution)/shard_map/psum | solution.py:217
  196.1 46.8 %all-gather.13.cloned.1.call-done = bf16[8192,2,64]{0,2,1:T(8,128)(2,1)} async-done(((bf16[1024,2,64]{0,2,1:T(8,128)(2,1)}), bf16[8192,2,64]{0,2,1:T(8,128)(2,1)}) %all-gather.13.cloned.1.call-update) | async-done | bytes 2097168 | tf_op jit(solution)/shard_map/all_gather | solution.py:262
  242.9 50.6 %all-gather.11.cloned.1.call-done = bf16[8192,2,64]{0,2,1:T(8,128)(2,1)} async-done(((bf16[1024,2,64]{0,2,1:T(8,128)(2,1)}), bf16[8192,2,64]{0,2,1:T(8,128)(2,1)}) %all-gather.11.cloned.1.call-update) | async-done | bytes 2097168 | tf_op jit(solution)/shard_map/all_gather | solution.py:261
  294.1 132.3 %while.52 = (s32[]{:T(128)}, f32[2,1024]{1,0:T(2,128)}, f32[2,1024]{1,0:T(2,128)}, f32[2,1024,64]{1,2,0:T(8,128)}, s32[1024]{0:T(1024)}, /*index=5*/s32[8]{0:T(1...) while((s32[]{:T(128)}, f32[2,1024]{1,0:T(2,128)}, ...), condition=%wide.region_19.20_spmd.clone, body=%wide.region_16.19_spmd.clone.sunk | while | flops 1905666048 | bytes 35635560 | solution.py:166
  303.4 6.5 fusion.241
  319.9 6.5 fusion.241
  336.4 6.5 fusion.241
  352.9 6.5 fusion.241
  369.4 6.5 fusion.241
  386.0 6.5 fusion.241
  402.5 6.5 fusion.241
  419.0 6.5 fusion.241
  436.5 27.9 %all-reduce.14.cloned.1.call-done = bf16[1024,512]{1,0:T(8,128)(2,1)} async-done(((bf16[1024,512]{1,0:T(8,128)(2,1)}), bf16[1024,512]{1,0:T(8,128)(2,1)}) %all-reduce.14.cloned.1.call-update) | async-done | bytes 1048592 | tf_op jit(solution)/shard_map/psum | solution.py:217
  473.8 22.0 %psum.70 = f32[3]{0:T(128)} all-reduce(f32[3]{0:T(128)} %get-tuple-element.566), channel_id=1, replica_groups=mesh['blk'=8,'head'=4] {'blk'}, use_global_device_ids=true, to_apply=%region_10.11 | all-reduce | flops 3 | bytes 24 | tf_op jit(solution)/shard_map/psum | solution.py:289
  516.5 5.2 all-gather.2
  524.2 5.4 all-gather
  532.1 5.4 all-gather.1
  540.0 12.1 while.51
  557.7 36.5 %all-reduce.18.cloned.1.call-done = bf16[1024,512]{1,0:T(8,128)(2,1)} async-done(((bf16[1024,512]{1,0:T(8,128)(2,1)}), bf16[1024,512]{1,0:T(8,128)(2,1)}) %all-reduce.18.cloned.1.call-update) | async-done | bytes 1048592 | tf_op jit(solution)/shard_map/psum | solution.py:217
  607.8 33.4 %all-reduce.20.cloned.1.call-done = bf16[1024,512]{1,0:T(8,128)(2,1)} async-done(((bf16[1024,512]{1,0:T(8,128)(2,1)}), bf16[1024,512]{1,0:T(8,128)(2,1)}) %all-reduce.20.cloned.1.call-update) | async-done | bytes 1048592 | tf_op jit(solution)/shard_map/psum | solution.py:217
  650.8 171.3 %while.53 = (s32[]{:T(128)}, f32[1024,2,64]{0,2,1:T(8,128)}, bf16[8,1024,2,64]{1,3,2,0:T(8,128)(2,1)}, bf16[8,1024,2,64]{1,3,2,0:T(8,128)(2,1)}, s32[8]{0:T(128)...) while((s32[]{:T(128)}, f32[1024,2,64]{0,2,1:T(8,128)}, ...), condition=%wide.region_40.41_spmd.clone, body=%wide.region_38.40_spmd.clone.sunk | while | flops 2706917376 | bytes 50180516 | solution.py:335
  656.6 7.1 fusion.255
  663.7 4.5 fusion.252
  678.0 7.1 fusion.255
  685.1 4.5 fusion.252
  699.4 7.1 fusion.255
  706.5 4.5 fusion.252
  720.7 7.1 fusion.255
  727.9 4.5 fusion.252
  742.1 7.1 fusion.255
  749.2 4.5 fusion.252
  763.5 7.1 fusion.255
  770.6 4.5 fusion.252
  784.9 7.1 fusion.255
  792.0 4.5 fusion.252
  806.3 7.1 fusion.255
  845.5 51.0 %reduce-scatter.5.cloned.1.call-done = bf16[1024,128]{0,1:T(8,128)(2,1)} async-done(((bf16[8192,128]{0,1:T(8,128)(2,1)}), bf16[1024,128]{0,1:T(8,128)(2,1)}) %reduce-scatter.5.cloned.1.call-update) | async-done | bytes 262160 | tf_op jit(solution)/shard_map/reduce_scatter | solution.py:343
  896.5 71.1 %reduce-scatter.3.cloned.1.call-done = bf16[1024,128]{0,1:T(8,128)(2,1)} async-done(((bf16[8192,128]{0,1:T(8,128)(2,1)}), bf16[1024,128]{0,1:T(8,128)(2,1)}) %reduce-scatter.3.cloned.1.call-update) | async-done | bytes 262160 | tf_op jit(solution)/shard_map/reduce_scatter | solution.py:337
  986.5 19.2 %all-reduce.22.cloned.1.call-done = bf16[1024,512]{1,0:T(8,128)(2,1)} async-done(((bf16[1024,512]{1,0:T(8,128)(2,1)}), bf16[1024,512]{1,0:T(8,128)(2,1)}) %all-reduce.22.cloned.1.call-update) | async-done | bytes 1048592 | tf_op jit(solution)/shard_map/psum | solution.py:217
  1032.2 29.3 %all-reduce.24.cloned.1.call-done = bf16[1024,512]{1,0:T(8,128)(2,1)} async-done(((bf16[1024,512]{1,0:T(8,128)(2,1)}), bf16[1024,512]{1,0:T(8,128)(2,1)}) %all-reduce.24.cloned.1.call-update) | async-done | bytes 1048592 | tf_op jit(solution)/shard_map/psum | solution.py:217
  1065.1 9.5 scatter_custom_fusion
  1080.6 156.0 %all-reduce.26.cloned.1.call-done = (bf16[1187840]{0:T(1024)(128)(2,1)}, bf16[928768]{0:T(1024)(128)(2,1)}) async-done(((bf16[1187840]{0:T(1024)(128)(2,1)}, bf16[928768]{0:T(1024)(128)(2,1)}), (bf16[1187840]{0:T(1024)(128)(2,1)}, bf16[928768]{0:T(1024)(128)(2,1)})) %all-reduce.26.cloned.1.call-update) | async-done | bytes 4233232
  1241.3 19.6 %psum.79 = f32[3]{0:T(128)} all-reduce(f32[3]{0:T(128)S(1)} %copy-done.138), channel_id=1, replica_groups=mesh['blk'=8,'head'=4] {'blk'}, use_global_device_ids=true, to_apply=%region_60.61 | all-reduce | flops 3 | bytes 24 | tf_op jit(solution)/shard_map/psum | solution.py:289
  1260.9 36.8 %psum.78 = f32[]{:T(128)} all-reduce(f32[]{:T(128)S(6)} %add.346), channel_id=1, replica_groups=mesh['blk'=8,'head'=4] {'blk','head'}, use_global_device_ids=true, to_apply=%region_58.59 | all-reduce | flops 1 | bytes 8 | tf_op jit(solution)/shard_map/psum | solution.py:416
  (755 shorter events, 360.1 us)
Async XLA Ops:
  7.2 504.5 %copy-start = (bf16[1024,1026]{0,1:T(8,128)(2,1)S(1)}, bf16[1024,1026]{0,1:T(8,128)(2,1)}, u32[]{:S(2)}) copy-start(bf16[1024,1026]{0,1:T(8,128)(2,1)} %param.19) | copy-start | bytes 6303748
  7.2 73.7 %all-gather.15.cloned.1.call-start = ((), (), s32[]{:S(2)}) async-start(), calls=%async_computation.14 | async-start | bytes 4179456 | tf_op jit(solution)/shard_map/all_gather | solution.py:221
  9.5 128.0 %all-gather.9.cloned.1.call-start = ((), (), s32[]{:S(2)}) async-start(), calls=%async_computation.2 | async-start | bytes 2672640 | tf_op jit(solution)/shard_map/all_gather | solution.py:220
  11.4 175.8 %all-reduce.12.cloned.1.call-start = ((), (), s32[]{:S(2)}) async-start(), calls=%async_computation.3 | async-start | bytes 2097152 | tf_op jit(solution)/shard_map/psum | solution.py:217
  11.7 109.9 %copy-start.57 = (s32[1024]{0:T(1024)}, s32[1024]{0:T(1024)S(1)}, u32[]{:S(2)}) copy-start(s32[1024]{0:T(1024)S(1)} %convert_reduce_fusion.4) | copy-start | bytes 12292
  12.4 129.4 %copy-start.125 = (f32[512]{0:T(512)}, f32[512]{0:T(512)S(1)}, u32[]{:S(2)}) copy-start(f32[512]{0:T(512)S(1)} %broadcast_multiply_fusion.4) | copy-start | bytes 6148
  12.6 129.1 %copy-start.137 = (f32[512]{0:T(512)}, f32[512]{0:T(512)S(1)}, u32[]{:S(2)}) copy-start(f32[512]{0:T(512)S(1)} %add_rsqrt_fusion) | copy-start | bytes 6148
  135.7 8.0 copy-start.76
  136.9 6.7 copy-start.105
  137.5 6.1 copy-start.108
  152.5 90.4 %all-gather.13.cloned.1.call-start = ((), (), s32[]{:S(2)}) async-start(), calls=%async_computation.5 | async-start | bytes 2359296 | tf_op jit(solution)/shard_map/all_gather | solution.py:262
  153.5 36.6 %copy-start.93 = (f32[512]{0:T(512)S(1)}, f32[512]{0:T(512)}, u32[]{:S(2)}) copy-start(f32[512]{0:T(512)} %get-tuple-element.591) | copy-start | bytes 6148
  193.1 100.4 %all-gather.11.cloned.1.call-start = ((), (), s32[]{:S(2)}) async-start(), calls=%async_computation.4 | async-start | bytes 2359296 | tf_op jit(solution)/shard_map/all_gather | solution.py:261
  193.7 270.7 %all-reduce.14.cloned.1.call-start = ((), (), s32[]{:S(2)}) async-start(), calls=%async_computation.6 | async-start | bytes 2097152 | tf_op jit(solution)/shard_map/psum | solution.py:217
  303.4 6.6 copy-start.59
  319.9 6.6 copy-start.59
  336.4 6.6 copy-start.59
  352.9 6.6 copy-start.59
  369.4 6.6 copy-start.59
  385.9 6.6 copy-start.59
  402.5 6.6 copy-start.59
  419.0 6.6 copy-start.59
  429.7 78.8 %all-reduce.16.cloned.1.call-start = ((), (), s32[]{:S(2)}) async-start(), calls=%async_computation.7 | async-start | bytes 2097152 | tf_op jit(solution)/shard_map/psum | solution.py:217
  471.9 122.4 %all-reduce.18.cloned.1.call-start = ((), (), s32[]{:S(2)}) async-start(), calls=%async_computation.8 | async-start | bytes 2097152 | tf_op jit(solution)/shard_map/psum | solution.py:217
  557.7 83.6 %all-reduce.20.cloned.1.call-start = ((), (), s32[]{:S(2)}) async-start(), calls=%async_computation.9 | async-start | bytes 2097152 | tf_op jit(solution)/shard_map/psum | solution.py:217
  604.6 291.9 %reduce-scatter.5.cloned.1.call-start = ((), (), s32[]{:S(2)}) async-start(), calls=%async_computation.11 | async-start | bytes 2359296 | tf_op jit(solution)/shard_map/reduce_scatter | solution.py:343
  656.6 7.1 copy-start.124
  678.0 7.1 copy-start.124
  699.4 7.1 copy-start.124
  720.7 7.1 copy-start.124
  742.1 7.1 copy-start.124
  763.5 7.1 copy-start.124
  784.9 7.1 copy-start.124
  806.3 7.1 copy-start.124
  827.6 140.0 %reduce-scatter.3.cloned.1.call-start = ((), (), s32[]{:S(2)}) async-start(), calls=%async_computation.10 | async-start | bytes 2359296 | tf_op jit(solution)/shard_map/reduce_scatter | solution.py:337
  833.2 172.5 %all-reduce.22.cloned.1.call-start = ((), (), s32[]{:S(2)}) async-start(), calls=%async_computation.12 | async-start | bytes 2097152 | tf_op jit(solution)/shard_map/psum | solution.py:217
  842.9 124.7 %copy-start.69 = (bf16[512,384]{1,0:T(8,128)(2,1)S(1)}, bf16[512,384]{1,0:T(8,128)(2,1)}, u32[]{:S(2)}) copy-start(bf16[512,384]{1,0:T(8,128)(2,1)} %reshape.507) | copy-start | bytes 1179652
  970.5 91.1 %all-reduce.24.cloned.1.call-start = ((), (), s32[]{:S(2)}) async-start(), calls=%async_computation.13 | async-start | bytes 2097152 | tf_op jit(solution)/shard_map/psum | solution.py:217
  974.8 7.4 copy-start.132
  974.8 7.9 copy-start.31
  1024.9 211.7 %all-reduce.26.cloned.1.call-start = ((), (), s32[]{:S(2)}) async-start(), calls=%async_computation.15 | async-start | bytes 8466432
  1026.9 5.3 copy-start.133
  1029.8 33.6 %copy-start.99 = (f32[1024]{0:T(1024)S(1)}, f32[1024]{0:T(1024)}, u32[]{:S(2)}) copy-start(f32[1024]{0:T(1024)} %copy-done.98) | copy-start | bytes 12292
  1029.8 33.7 %copy-start.78 = (f32[1024]{0:T(1024)S(1)}, f32[1024]{0:T(1024)}, u32[]{:S(2)}) copy-start(f32[1024]{0:T(1024)} %copy-done.76) | copy-start | bytes 12292
  1029.8 33.7 %copy-start.107 = (f32[1024]{0:T(1024)S(1)}, f32[1024]{0:T(1024)}, u32[]{:S(2)}) copy-start(f32[1024]{0:T(1024)} %copy-done.105) | copy-start | bytes 12292
  1029.8 33.7 %copy-start.110 = (f32[512]{0:T(512)S(1)}, f32[512]{0:T(512)}, u32[]{:S(2)}) copy-start(f32[512]{0:T(512)} %copy-done.108) | copy-start | bytes 6148
  1078.1 163.3 %copy-start.138 = (f32[3]{0:T(128)S(1)}, f32[3]{0:T(128)}, u32[]{:S(2)}) copy-start(f32[3]{0:T(128)} %get-tuple-element.488) | copy-start | bytes 40
  1078.1 220.4 %copy-start.29 = (f32[148480]{0:T(1024)S(1)}, f32[148480]{0:T(1024)}, u32[]{:S(2)}) copy-start(f32[148480]{0:T(1024)} %param.24) | copy-start | bytes 1781764
  (182 other events, 433.9 us)
Sparse Core Ops, SparseCore 0:
  10.8 70.0 all-gather.14
  83.7 50.7 all-gather.8
  152.6 34.4 all-reduce.11
  193.2 49.6 all-gather.12
  245.8 47.7 all-gather.10
  429.8 34.5 all-reduce.13
  472.0 36.4 all-reduce.15
  557.8 36.4 all-reduce.17
  604.7 36.4 all-reduce.19
  827.7 68.7 reduce-scatter.4
  900.5 67.0 reduce-scatter.2
  970.6 35.0 all-reduce.21
  1025.0 36.4 all-reduce.23
  1078.2 158.2 all-reduce.25
where the time goes:
time: 1330 us; the launch traced here: 1310 us
  waiting for transfers between devices  626 us (47%)
  matrix products  269 us (20%)
  other arithmetic  163 us (12%)
  local copies, waits for them, and re-layouts  125 us (9%)
  blocking collectives  94.2 us (7%)
  between operations  20.4 us (2%)
    psum x7, waiting for transfers between devices, over_heads(): return lax.psum(x.astype(jnp.bfloat16), 'head').astype(jnp.float32)  182 us
    unnamed x15, waiting for transfers between devices  157 us
    reduce_scatter x1, waiting for transfers between devices, per_device(): lax.psum_scatter(key_parts[0].reshape(amount_all, width).astype(jnp.bfloa...  71.1 us
    all_gather x1, waiting for transfers between devices, per_device(): lax.all_gather(common_params.astype(jnp.bfloat16), 'blk', axis=0, tiled=T...  67.6 us
    dot_general x9, matrix products, block_grads(): jnp.einsum('hqk,qhd->khd', probs, dout.astype(jnp.float32), precision=hig...  60.2 us
    dot_general x8, matrix products, one_block(): jnp.einsum('hqk,khd->hqd', probs, block_values, precision=highest)  52.3 us
    reduce_scatter x1, waiting for transfers between devices, per_device(): lax.psum_scatter(key_parts[1].reshape(amount_all, width).astype(jnp.bfloa...  51 us
    all_gather x1, waiting for transfers between devices, per_device(): lax.all_gather(keys_self, 'blk', axis=0, tiled=True)  50.6 us
  transfers between devices with their start and end apart: 14, of which 13 were waited for; matrix products, arithmetic and copies ran while one was open for 9% of the time, Pallas kernels for 0%

commit v1 on v0

v1 whole, which is shorter than its diff:
```python
import functools

import jax
import jax.numpy as jnp
from jax import lax
from jax.experimental import pallas as pl
from jax.experimental.pallas import tpu as pltpu
from jax.sharding import PartitionSpec as P

D = 512
HEADS = 8
HD = 64
FF = 2048
DI = 704
DQ = 1026
C = 704
LAT = 784
MODES = 3
STEP = 10
LANES = 128
TILE = 16

norm_eps = 1e-05
learn_rate = 0.1
beta_one = 0.9
beta_two = 0.999
adam_eps = 1e-08
weight_decay = 0.01
clip_limit = 0.05
big_negative = -1e30
low = jnp.bfloat16
MESH = pl.DeviceIdType.MESH
MIB = 1 << 20


def round_up(n, unit):
    return -(-n // unit) * unit


def grid_of(n_blk, n_head):
    cores = 2 if n_head % 2 == 0 else 1
    x = n_head // cores
    y = x if n_blk % x == 0 else 1
    return (n_blk // y, y, x, cores)


def my_place(dims):
    blk, head = lax.axis_index("blk"), lax.axis_index("head")
    return (blk // dims[1], lax.rem(blk, dims[1]), head // dims[3], lax.rem(head, dims[3]))


def shifted(dims, me, offset, sign):
    return tuple(
        m if o == 0 else lax.rem(m + (o if sign > 0 else n - o), n)
        for m, o, n in zip(me, offset, dims)
    )


def blk_of(dims, place):
    return place[0] * dims[1] + place[1]


def head_of(dims, place):
    return place[2] * dims[3] + place[3]


def device_of(dims, place):
    return {"blk": blk_of(dims, place), "head": head_of(dims, place)}


def along(axis, d):
    return tuple(d if a == axis else 0 for a in range(4))


def greet(dims, me, offsets):
    barrier = pltpu.get_barrier_semaphore()
    for offset in offsets:
        pl.semaphore_signal(
            barrier,
            inc=1,
            device_id=device_of(dims, shifted(dims, me, offset, 1)),
            device_id_type=MESH,
        )
    pl.semaphore_wait(barrier, len(offsets))


def axis_peers(dims, axes):
    return [along(axis, d) for axis in axes for d in range(1, dims[axis])]


def remote(src, dst, send_sem, recv_sem, place, dims):
    return pltpu.make_async_remote_copy(
        src_ref=src,
        dst_ref=dst,
        send_sem=send_sem,
        recv_sem=recv_sem,
        device_id=device_of(dims, place),
        device_id_type=MESH,
    )


def gather_plan(dims, parts):
    plan = []
    for position in range(4):
        for p, (first, rows, order) in enumerate(parts):
            axis = order[position]
            done = order[:position]
            offsets = [(0, 0, 0, 0)]
            for a in done:
                offsets = [
                    tuple(d if i == a else o[i] for i in range(4))
                    for d in range(dims[a])
                    for o in offsets
                ]
            for d in range(1, dims[axis]):
                for o in offsets:
                    plan.append((p, tuple(d if i == axis else o[i] for i in range(4)), position))
    return plan


def gather_kernel(dims, parts, src, out, send_sem, recv_sem, own_sem):
    me = my_place(dims)
    plan = gather_plan(dims, parts)
    number = {(p, offset): i for i, (p, offset, position) in enumerate(plan)}
    axes = [a for a in range(4) if dims[a] > 1]
    greet(dims, me, axis_peers(dims, axes))
    own = pltpu.make_async_copy(src, out.at[blk_of(dims, me), head_of(dims, me)], own_sem)
    own.start()
    started = []

    def block(p, offset):
        place = shifted(dims, me, offset, -1)
        first, rows, order = parts[p]
        return out.at[blk_of(dims, place), head_of(dims, place), pl.ds(first, rows)]

    def forward(p, offset, position):
        first, rows, order = parts[p]
        source = src.at[pl.ds(first, rows)] if position < 0 else block(p, offset)
        for axis in order[position + 1 :]:
            for d in range(1, dims[axis]):
                i = number[(p, tuple(d if a == axis else offset[a] for a in range(4)))]
                copy = remote(
                    source,
                    block(p, offset),
                    send_sem.at[i],
                    recv_sem.at[i],
                    shifted(dims, me, along(axis, d), 1),
                    dims,
                )
                copy.start()
                started.append(copy)

    for p in range(len(parts)):
        forward(p, (0, 0, 0, 0), -1)
    for i, (p, offset, position) in enumerate(plan):
        landed = block(p, offset)
        axis = parts[p][2][position]
        remote(
            landed,
            landed,
            send_sem.at[i],
            recv_sem.at[i],
            shifted(dims, me, along(axis, offset[axis]), -1),
            dims,
        ).wait_recv()
        forward(p, offset, position)
    for copy in started:
        copy.wait_send()
    own.wait()


def gather_all(dims, shard, collective_id):
    rows = shard.shape[0]
    first = rows // 2 // TILE * TILE
    parts = ((0, first, (0, 1, 2, 3)), (first, rows - first, (0, 2, 1, 3)))
    count = len(gather_plan(dims, parts))
    z, y, x, cores = dims
    return pl.pallas_call(
        functools.partial(gather_kernel, dims, parts),
        out_shape=jax.ShapeDtypeStruct((z * y, x * cores) + shard.shape, shard.dtype),
        in_specs=[pl.BlockSpec(memory_space=pl.ANY)],
        out_specs=pl.BlockSpec(memory_space=pl.ANY),
        scratch_shapes=[
            pltpu.SemaphoreType.DMA((count,)),
            pltpu.SemaphoreType.DMA((count,)),
            pltpu.SemaphoreType.DMA(()),
        ],
        compiler_params=pltpu.CompilerParams(collective_id=collective_id, has_side_effects=True),
        name="gather_weights",
    )(shard)


def reduce_plan(dims, order):
    stages = []
    for position, axis in enumerate(order):
        rest = order[position + 1 :]
        offsets = [(0, 0, 0, 0)]
        for a in reversed(rest):
            offsets = [
                tuple(d if i == a else o[i] for i in range(4))
                for d in list(range(1, dims[a])) + [0]
                for o in offsets
            ]
        stages.append((axis, offsets))
    return stages


def reduce_kernel(dims, parts, chunk, src, out, *scratch):
    me = my_place(dims)
    places = len(parts) * 4
    buffers, send_sem, recv_sem = scratch[:places], scratch[places], scratch[places + 1]
    axes = [a for a in range(4) if dims[a] > 1]
    greet(dims, me, axis_peers(dims, axes))
    started = []
    numbers = [0]
    pending = {}

    def source(p, position, offset):
        first, rows, order = parts[p]
        if position == 0:
            place = shifted(dims, me, offset, 1)
            return src.at[blk_of(dims, place), head_of(dims, place), pl.ds(first, rows)]
        k = stages[p][position - 1][1].index(offset)
        return buffers[p * 4 + position - 1].at[k, 0]

    stages = [reduce_plan(dims, order) for first, rows, order in parts]

    def send(p, position, k, d):
        axis, offsets = stages[p][position]
        i = numbers[0]
        numbers[0] += 1
        there = tuple(d if a == axis else offsets[k][a] for a in range(4))
        copy = remote(
            source(p, position, there),
            buffers[p * 4 + position].at[k, d - 1],
            send_sem.at[i],
            recv_sem.at[i],
            shifted(dims, me, along(axis, d), 1),
            dims,
        )
        copy.start()
        started.append(copy)
        pending[(p, position, k, d)] = copy

    def add(p, position, k):
        first, rows, order = parts[p]
        axis, offsets = stages[p][position]
        for d in range(1, dims[axis]):
            pending[(p, position, k, d)].wait_recv()
        mine = source(p, position, offsets[k])
        arrived = buffers[p * 4 + position]
        step = chunk(rows)
        last = position == 3

        @pl.loop(0, rows // step)
        def some_rows(n):
            at = pl.ds(pl.multiple_of(n * step, step), step)
            total = mine[at].astype(jnp.float32)
            for d in range(1, dims[axis]):
                total = total + arrived[k, d - 1, at].astype(jnp.float32)
            if last:
                out[pl.ds(pl.multiple_of(first + n * step, TILE), step)] = total
            else:
                arrived[k, 0, at] = total.astype(low)

    for position in range(4):
        for k in range(len(stages[0][position][1])):
            for p in range(len(parts)):
                if position == 0:
                    for d in range(1, dims[stages[p][0][0]]):
                        send(p, 0, k, d)
        for k in range(len(stages[0][position][1])):
            for p in range(len(parts)):
                add(p, position, k)
                if position < 3:
                    axis, offsets = stages[p][position + 1]
                    offset = stages[p][position][1][k]
                    rest = tuple(0 if a == axis else offset[a] for a in range(4))
                    if offset[axis]:
                        send(p, position + 1, offsets.index(rest), offset[axis])
    for copy in started:
        copy.wait_send()


def row_chunk(rows):
    for count in (4, 3, 2):
        if rows % (count * TILE) == 0:
            return rows // count
    return rows


def reduce_all(dims, blocks, collective_id):
    rows = blocks.shape[2]
    first = rows // 2 // TILE * TILE
    parts = ((0, first, (3, 2, 1, 0)), (first, rows - first, (3, 1, 2, 0)))
    scratch = []
    count = 0
    for start, amount, order in parts:
        for axis, offsets in reduce_plan(dims, order):
            others = max(dims[axis] - 1, 1)
            count += len(offsets) * (dims[axis] - 1)
            scratch.append(pltpu.VMEM((len(offsets), others, amount, LANES), low))
    return pl.pallas_call(
        functools.partial(reduce_kernel, dims, parts, row_chunk),
        out_shape=jax.ShapeDtypeStruct((rows, LANES), jnp.float32),
        in_specs=[pl.BlockSpec(memory_space=pltpu.VMEM)],
        out_specs=pl.BlockSpec(memory_space=pltpu.VMEM),
        scratch_shapes=scratch
        + [pltpu.SemaphoreType.DMA((count,)), pltpu.SemaphoreType.DMA((count,))],
        compiler_params=pltpu.CompilerParams(
            collective_id=collective_id, has_side_effects=True, vmem_limit_bytes=56 * MIB
        ),
        name="reduce_gradients",
    )(blocks)


def spread_kernel(dims, q_in, kv_in, q_out, kv_out, send_sem, recv_sem, own_sem):
    z, y, x, cores = dims
    me = my_place(dims)
    heads = x * cores
    my_blk, my_head = blk_of(dims, me), head_of(dims, me)
    across = [(0, 0, a, c) for a in range(x) for c in range(cores) if (a, c) != (0, 0)]
    across.sort(key=lambda o: (o[2] == 0, o[3]))
    ups = [along(0, d) for d in range(1, z)]
    sides = [along(1, d) for d in range(1, y)]
    greet(dims, me, across + ups + sides)
    own_q = pltpu.make_async_copy(q_in.at[my_head], q_out.at[my_head], own_sem.at[0])
    own_kv = pltpu.make_async_copy(kv_in.at[my_head], kv_out.at[my_blk, my_head], own_sem.at[1])
    own_kv.start()
    own_q.start()
    started = []
    count = [0]

    def push(src, dst, place):
        i = count[0]
        count[0] += 1
        copy = remote(src, dst, send_sem.at[i], recv_sem.at[i], place, dims)
        copy.start()
        started.append(copy)
        return copy

    landed_kv = []
    for o in across:
        place = shifted(dims, me, o, 1)
        landed_kv.append(push(kv_in.at[head_of(dims, place)], kv_out.at[my_blk, my_head], place))
    landed_q = []
    for o in across:
        place = shifted(dims, me, o, 1)
        landed_q.append(push(q_in.at[head_of(dims, place)], q_out.at[my_head], place))
    pieces = [(0, 0, 0, 0)] + across
    up_copies = {}
    side_copies = {}

    def kv_block(place_blk, offset):
        place = shifted(dims, me, offset, -1)
        return kv_out.at[place_blk, head_of(dims, place)]

    def spread_own(n):
        block = kv_block(my_blk, pieces[n])
        for o in ups:
            up_copies[(n, o)] = push(block, block, shifted(dims, me, o, 1))
        for o in sides:
            side_copies[(n, along(0, 0), o)] = push(block, block, shifted(dims, me, o, 1))

    own_kv.wait()
    spread_own(0)
    order = sorted(range(1, len(pieces)), key=lambda n: (pieces[n][2] != 0, pieces[n][3]))
    for n in order:
        landed_kv[n - 1].wait_recv()
        spread_own(n)
    for u in ups:
        for n in [0] + order:
            up_copies[(n, u)].wait_recv()
            block = kv_block(blk_of(dims, shifted(dims, me, u, -1)), pieces[n])
            for o in sides:
                side_copies[(n, u, o)] = push(block, block, shifted(dims, me, o, 1))
    for copy in landed_q:
        copy.wait_recv()
    for copy in side_copies.values():
        copy.wait_recv()
    for copy in started:
        copy.wait_send()
    own_q.wait()


def spread_rows(dims, q, kv, collective_id):
    z, y, x, cores = dims
    heads = x * cores
    count = 2 * (heads - 1) + heads * (z - 1 + z * (y - 1))
    return pl.pallas_call(
        functools.partial(spread_kernel, dims),
        out_shape=(
            jax.ShapeDtypeStruct(q.shape, low),
            jax.ShapeDtypeStruct((z * y,) + kv.shape, low),
        ),
        in_specs=[pl.BlockSpec(memory_space=pl.ANY)] * 2,
        out_specs=[pl.BlockSpec(memory_space=pl.ANY)] * 2,
        scratch_shapes=[
            pltpu.SemaphoreType.DMA((count,)),
            pltpu.SemaphoreType.DMA((count,)),
            pltpu.SemaphoreType.DMA((2,)),
        ],
        compiler_params=pltpu.CompilerParams(collective_id=collective_id, has_side_effects=True),
        name="spread_rows",
    )(q, kv)


def swap_kernel(dims, src, out, send_sem, recv_sem, own_sem):
    z, y, x, cores = dims
    me = my_place(dims)
    my_head = head_of(dims, me)
    across = [(0, 0, a, c) for a in range(x) for c in range(cores) if (a, c) != (0, 0)]
    greet(dims, me, across)
    copies = []
    for i, o in enumerate(across):
        place = shifted(dims, me, o, 1)
        copy = remote(
            src.at[head_of(dims, place)], out.at[my_head], send_sem.at[i], recv_sem.at[i], place, dims
        )
        copy.start()
        copies.append(copy)
    own = pltpu.make_async_copy(src.at[my_head], out.at[my_head], own_sem)
    own.start()
    for copy in copies:
        copy.wait_recv()
    for copy in copies:
        copy.wait_send()
    own.wait()


def swap_heads(dims, blocks, collective_id):
    count = dims[2] * dims[3] - 1
    return pl.pallas_call(
        functools.partial(swap_kernel, dims),
        out_shape=jax.ShapeDtypeStruct(blocks.shape, blocks.dtype),
        in_specs=[pl.BlockSpec(memory_space=pl.ANY)],
        out_specs=pl.BlockSpec(memory_space=pl.ANY),
        scratch_shapes=[
            pltpu.SemaphoreType.DMA((count,)),
            pltpu.SemaphoreType.DMA((count,)),
            pltpu.SemaphoreType.DMA(()),
        ],
        compiler_params=pltpu.CompilerParams(collective_id=collective_id, has_side_effects=True),
        name="swap_heads",
    )(blocks)


def collect_kernel(dims, src, out, side_buf, up_buf, send_sem, recv_sem):
    z, y, x, cores = dims
    me = my_place(dims)
    greet(dims, me, axis_peers(dims, (0, 1)))
    started = []
    rows = src.shape[1]
    step = 256

    def push(s, dst, place):
        i = len(started)
        copy = remote(s, dst, send_sem.at[i], recv_sem.at[i], place, dims)
        copy.start()
        started.append(copy)
        return copy

    side = {}
    for u in list(range(1, z)) + [0]:
        for d in range(1, y):
            place = shifted(dims, me, (u, d, 0, 0), 1)
            side[(u, d)] = push(
                src.at[blk_of(dims, place)], side_buf.at[u, d - 1], shifted(dims, me, along(1, d), 1)
            )
    up = {}
    for u in list(range(1, z)) + [0]:
        for d in range(1, y):
            side[(u, d)].wait_recv()
        mine = src.at[blk_of(dims, shifted(dims, me, along(0, u), 1))]

        @pl.loop(0, rows // step)
        def some_rows(n):
            at = pl.ds(pl.multiple_of(n * step, step), step)
            total = mine[at].astype(jnp.float32)
            for d in range(1, y):
                total = total + side_buf[u, d - 1, at].astype(jnp.float32)
            side_buf[u, 0, at] = total.astype(low)

        if u:
            up[u] = push(
                side_buf.at[u, 0], up_buf.at[u - 1], shifted(dims, me, along(0, u), 1)
            )
    for u in range(1, z):
        up[u].wait_recv()

    @pl.loop(0, rows // step)
    def last_rows(n):
        at = pl.ds(pl.multiple_of(n * step, step), step)
        total = side_buf[0, 0, at].astype(jnp.float32)
        for u in range(1, z):
            total = total + up_buf[u - 1, at].astype(jnp.float32)
        out[at] = total.astype(low)

    for copy in started:
        copy.wait_send()


def collect_rows(dims, parts, collective_id):
    z, y, x, cores = dims
    shape = parts.shape[1:]
    count = z * (y - 1) + z - 1
    return pl.pallas_call(
        functools.partial(collect_kernel, dims),
        out_shape=jax.ShapeDtypeStruct(shape, low),
        in_specs=[pl.BlockSpec(memory_space=pltpu.VMEM)],
        out_specs=pl.BlockSpec(memory_space=pltpu.VMEM),
        scratch_shapes=[
            pltpu.VMEM((z, max(y - 1, 1)) + shape, low),
            pltpu.VMEM((max(z - 1, 1),) + shape, low),
            pltpu.SemaphoreType.DMA((count,)),
            pltpu.SemaphoreType.DMA((count,)),
        ],
        compiler_params=pltpu.CompilerParams(
            collective_id=collective_id, has_side_effects=True, vmem_limit_bytes=48 * MIB
        ),
        name="collect_rows",
    )(parts)


def contract_first(a, b):
    return lax.dot_general(a, b, (((0,), (0,)), ((), ())), preferred_element_type=jnp.float32)


def product(a, b):
    return jnp.dot(a, b, preferred_element_type=jnp.float32)


def against(a, b):
    return lax.dot_general(a, b, (((1,), (1,)), ((), ())), preferred_element_type=jnp.float32)


def clip_borders(bounds, where):
    clips = bounds.shape[1]
    opening = jnp.zeros(where.shape, jnp.int32)
    ending = jnp.full(where.shape, 1 << 30, jnp.int32)
    for clip in range(clips):
        here = where == HD + clip
        opening = jnp.where(here, bounds[0, clip], opening)
        ending = jnp.where(here, bounds[1, clip], ending)
    return opening, ending


def extend_keys(bounds, heads, rows_at_once, kv, keys, values):
    width = heads * HD
    clips = bounds.shape[1]
    lane = lax.broadcasted_iota(jnp.int32, (1, LANES), 1)
    opening, ending = clip_borders(bounds, lane)
    ones = jnp.where((lane >= HD + clips) & (lane < HD + clips + 3), 1.0, 0.0)
    value_tail = jnp.where((lane >= HD) & (lane < HD + 3), 1.0, 0.0) + jnp.zeros(
        (rows_at_once, LANES), jnp.float32
    )

    @pl.loop(0, kv.shape[0] // rows_at_once)
    def some_rows(n):
        first = pl.multiple_of(n * rows_at_once, rows_at_once)
        at = pl.ds(first, rows_at_once)
        row = first + lax.broadcasted_iota(jnp.int32, (rows_at_once, LANES), 0)
        tail = jnp.where((row >= opening) & (row < ending), ones, big_negative)
        block = kv[at, :].astype(jnp.float32)
        for a in range(heads):
            for first_column, target, end in ((0, keys, tail), (width, values, value_tail)):
                columns = block[:, first_column + a * HD : first_column + (a + 1) * HD]
                target[a, at, :] = jnp.concatenate([columns, end[:, HD:]], 1).astype(low)


def extend_queries(bounds, first_row, heads, q_t, a, extra):
    clips = bounds.shape[1]
    amount = q_t.shape[1]
    place = HD + lax.broadcasted_iota(jnp.int32, (HD, 1), 0)
    opening, ending = clip_borders(bounds, place)
    row = first_row + lax.broadcasted_iota(jnp.int32, (1, amount), 1)
    is_clip = place < HD + clips
    tail = jnp.where(is_clip & (row >= opening) & (row < ending), 1.0, 0.0)
    if extra is not None:
        tail = tail + in_three(place - HD - clips, -extra)
    return jnp.concatenate([q_t[a * HD : (a + 1) * HD] * HD ** (-0.5), tail], 0).astype(low)


def in_three(place, value):
    top = value.astype(low).astype(jnp.float32)
    middle = (value - top).astype(low).astype(jnp.float32)
    bottom = value - top - middle
    return (
        jnp.where(place == 0, top, 0.0)
        + jnp.where(place == 1, middle, 0.0)
        + jnp.where(place == 2, bottom, 0.0)
    )


def attend_kernel(heads, key_step, query_step, bounds, q, kv, out, lse, out_t, keys, values, queries, top, accum):
    first_row = lax.axis_index("blk") * q.shape[0]
    amount, total_keys = q.shape[0], kv.shape[0]
    extend_keys(bounds, heads, key_step, kv, keys, values)
    q_t = q[...].astype(jnp.float32).T
    for a in range(heads):
        queries[a] = extend_queries(bounds, first_row, heads, q_t, a, None)

    @pl.loop(0, amount // query_step)
    def query_block(n):
        at = pl.ds(pl.multiple_of(n * query_step, query_step), query_step)
        top[...] = jnp.full(top.shape, -1e38, jnp.float32)
        accum[...] = jnp.zeros(accum.shape, jnp.float32)

        @pl.loop(0, total_keys // key_step)
        def key_block(k):
            rows = pl.ds(pl.multiple_of(k * key_step, key_step), key_step)
            for a in range(heads):
                scores = product(keys[a, rows, :], queries[a, :, at])
                old = top[a : a + 1, :]
                new = jnp.maximum(old, jnp.max(scores, 0, keepdims=True))
                probs = jnp.exp(scores - new).astype(low)
                top[a : a + 1, :] = new
                accum[a] = accum[a] * jnp.exp(old - new) + contract_first(values[a, rows, :], probs)

        for a in range(heads):
            total = accum[a, HD : HD + 1, :]
            out_t[a * HD : (a + 1) * HD, at] = accum[a, :HD, :] / total
            lse[a : a + 1, at] = top[a : a + 1, :] + jnp.log(total)

    out[...] = out_t[...].T.astype(low)


def attend(bounds, q, kv, heads):
    amount, width = q.shape
    total_keys = kv.shape[0]
    key_step, query_step = 1024, 256
    vmem = pl.BlockSpec(memory_space=pltpu.VMEM)
    return pl.pallas_call(
        functools.partial(attend_kernel, heads, key_step, query_step),
        out_shape=(
            jax.ShapeDtypeStruct((amount, width), low),
            jax.ShapeDtypeStruct((heads, amount), jnp.float32),
            jax.ShapeDtypeStruct((width, amount), jnp.float32),
        ),
        in_specs=[pl.BlockSpec(memory_space=pltpu.SMEM), vmem, vmem],
        out_specs=[vmem] * 3,
        scratch_shapes=[
            pltpu.VMEM((heads, total_keys, LANES), low),
            pltpu.VMEM((heads, total_keys, LANES), low),
            pltpu.VMEM((heads, LANES, amount), low),
            pltpu.VMEM((heads, query_step), jnp.float32),
            pltpu.VMEM((heads, LANES, query_step), jnp.float32),
        ],
        compiler_params=pltpu.CompilerParams(vmem_limit_bytes=56 * MIB),
        name="attend",
    )(bounds, q, kv)


def attend_back_kernel(
    heads, key_step, bounds, q, kv, dout, out_t, lse, d_q, d_kv, keys, values, queries, douts, d_q_t, q_rows, do_rows
):
    first_row = lax.axis_index("blk") * q.shape[0]
    amount, total_keys = q.shape[0], kv.shape[0]
    width = heads * HD
    extend_keys(bounds, heads, 1024, kv, keys, values)
    q_low = q[...].astype(jnp.float32)
    do_low = dout[...].astype(jnp.float32)
    q_t, do_t = q_low.T, do_low.T
    place = lax.broadcasted_iota(jnp.int32, (HD, 1), 0)
    lane = lax.broadcasted_iota(jnp.int32, (1, width), 1)
    for a in range(heads):
        mine = slice(a * HD, (a + 1) * HD)
        queries[a] = extend_queries(bounds, first_row, heads, q_t, a, lse[a : a + 1, :])
        delta = jnp.sum(do_t[mine] * out_t[mine, :], 0, keepdims=True)
        douts[a] = jnp.concatenate([do_t[mine], in_three(place, -delta)], 0).astype(low)
        here = (lane >= a * HD) & (lane < (a + 1) * HD)
        q_rows[a] = jnp.where(here, q_low * HD ** (-0.5), 0.0).astype(low)
        do_rows[a] = jnp.where(here, do_low, 0.0).astype(low)
    d_q_t[...] = jnp.zeros(d_q_t.shape, jnp.float32)

    @pl.loop(0, total_keys // key_step)
    def key_block(k):
        rows = pl.ds(pl.multiple_of(k * key_step, key_step), key_step)
        d_key = jnp.zeros((key_step, width), jnp.float32)
        d_value = jnp.zeros((key_step, width), jnp.float32)
        for a in range(heads):
            probs = jnp.exp(product(keys[a, rows, :], queries[a]))
            d_probs = product(values[a, rows, :], douts[a])
            d_scores = (probs * d_probs).astype(low)
            d_value = d_value + product(probs.astype(low), do_rows[a])
            d_key = d_key + product(d_scores, q_rows[a])
            d_q_t[a] = d_q_t[a] + contract_first(keys[a, rows, :], d_scores)
        d_kv[rows, :] = jnp.concatenate([d_key, d_value], 1).astype(low)

    whole = jnp.concatenate([d_q_t[a, :HD, :] for a in range(heads)], 0) * HD ** (-0.5)
    d_q[...] = whole.T.astype(low)


def attend_back(bounds, q, kv, dout, out_t, lse, heads):
    amount, width = q.shape
    total_keys = kv.shape[0]
    key_step = 256
    vmem = pl.BlockSpec(memory_space=pltpu.VMEM)
    return pl.pallas_call(
        functools.partial(attend_back_kernel, heads, key_step),
        out_shape=(
            jax.ShapeDtypeStruct((amount, width), low),
            jax.ShapeDtypeStruct((total_keys, 2 * width), low),
        ),
        in_specs=[pl.BlockSpec(memory_space=pltpu.SMEM)] + [vmem] * 5,
        out_specs=[vmem] * 2,
        scratch_shapes=[
            pltpu.VMEM((heads, total_keys, LANES), low),
            pltpu.VMEM((heads, total_keys, LANES), low),
            pltpu.VMEM((heads, LANES, amount), low),
            pltpu.VMEM((heads, LANES, amount), low),
            pltpu.VMEM((heads, LANES, amount), jnp.float32),
            pltpu.VMEM((heads, amount, width), low),
            pltpu.VMEM((heads, amount, width), low),
        ],
        compiler_params=pltpu.CompilerParams(vmem_limit_bytes=56 * MIB),
        name="attend_back",
    )(bounds, q, kv, dout, out_t, lse)


def layer_norm(x, gain):
    centre = x - jnp.mean(x, -1, keepdims=True)
    return centre * lax.rsqrt(jnp.mean(centre * centre, -1, keepdims=True) + norm_eps) * gain


def norm_pullback(x, gain, grad):
    unused, pull = jax.vjp(layer_norm, x, gain)
    return pull(grad)


def inner(a, b):
    return lax.dot_general(a, b, (((0,), (0,)), ((), ())), preferred_element_type=jnp.float32)


def part_shapes(n_head):
    width = HEADS // n_head * HD
    hidden = FF // n_head
    classes = C // n_head
    return (
        (D, width),
        (DI, 2 * width),
        (width, D),
        (D, 3 * width),
        (width, D),
        (D, hidden),
        (hidden, D),
        (D, classes),
    )


def adam_step(weight, first, second, grad):
    first = beta_one * first + (1 - beta_one) * grad
    second = beta_two * second + (1 - beta_two) * grad * grad
    fixed_first = first / (1 - beta_one**STEP)
    fixed_second = second / (1 - beta_two**STEP)
    weight = weight - learn_rate * (
        fixed_first / (jnp.sqrt(fixed_second) + adam_eps) + weight_decay * weight
    )
    return (weight, first, second, weight.astype(low))


def per_device(
    inputs,
    out_queries,
    clip_lengths,
    labels,
    modality,
    labeled,
    head_params,
    head_first,
    head_second,
    common_params,
    common_first,
    common_second,
):
    n_head, n_blk = lax.axis_size("head"), lax.axis_size("blk")
    dims = grid_of(n_blk, n_head)
    head_rank, blk_rank = lax.axis_index("head"), lax.axis_index("blk")
    blk_rows = labels.shape[0]
    rows = blk_rows // n_head
    heads_here = HEADS // n_head
    width = heads_here * HD
    n_h, n_c = head_params.shape[0], common_params.shape[0]
    head_rows = round_up(-(-n_h // LANES), TILE)
    piece_rows = round_up(-(-(-(-n_c // LANES)) // n_head), TILE)

    def mine(x):
        return lax.dynamic_slice_in_dim(x, head_rank * rows, rows, 0)

    head_low = jnp.pad(head_params.astype(low), (0, head_rows * LANES - n_h)).reshape(head_rows, LANES)
    common_low = jnp.pad(common_params.astype(low), (0, n_head * piece_rows * LANES - n_c))
    common_low = lax.dynamic_slice_in_dim(
        common_low.reshape(n_head * piece_rows, LANES), head_rank * piece_rows, piece_rows, 0
    )
    everything = gather_all(dims, jnp.concatenate([head_low, common_low], 0), 0)
    head_flat = [
        everything[:, g, :head_rows].reshape(n_blk, head_rows * LANES)[:, :n_h].reshape(-1)
        for g in range(n_head)
    ]
    common_flat = everything[:, :, head_rows:].reshape(n_blk, n_head * piece_rows * LANES)[:, :n_c]
    common_flat = common_flat.reshape(-1)
    shapes = part_shapes(n_head)
    parts = []
    border = 0
    for shape in shapes:
        amount = shape[0] * shape[1]
        parts.append([flat[border : border + amount].reshape(shape) for flat in head_flat])
        border += amount
    enc_query = jnp.concatenate(parts[0], 1)
    enc_key = jnp.concatenate([w[:, :width] for w in parts[1]], 1)
    enc_value = jnp.concatenate([w[:, width:] for w in parts[1]], 1)
    enc_output = jnp.concatenate(parts[2], 0)
    self_project = jnp.concatenate(parts[3], 1)
    self_output = jnp.concatenate(parts[4], 0)
    hidden_in = jnp.concatenate(parts[5], 1)
    hidden_out = jnp.concatenate(parts[6], 0)
    class_table = jnp.concatenate(parts[7], 1)
    query_table = common_flat[: DQ * D].reshape(DQ, D)
    latent_table = common_flat[DQ * D : (DQ + LAT) * D].reshape(LAT, D)
    norm_gains = common_flat[(DQ + LAT) * D :].reshape(4, D).astype(jnp.float32)

    finish = jnp.cumsum(clip_lengths)
    bounds = jnp.stack([finish - clip_lengths, finish])
    places = blk_rank * blk_rows + head_rank * rows + jnp.arange(rows, dtype=jnp.int32)
    inside = (places[:, None] >= bounds[0][None]) & (places[:, None] < bounds[1][None])
    offset = places - jnp.sum(jnp.where(inside, bounds[0][None], 0), 1)
    latent_rows = offset % LAT
    picked = (latent_rows[:, None] == jnp.arange(LAT, dtype=jnp.int32)[None]).astype(low)
    labels, modality, labeled = mine(labels), mine(modality), mine(labeled)
    out_queries = mine(out_queries)

    def split(x):
        return x.reshape(x.shape[0], HEADS, HD)

    z_zero = product(picked, latent_table)
    h_zero = layer_norm(z_zero, norm_gains[0]).astype(low)
    x_norm = layer_norm(inputs.astype(jnp.float32), 1.0).astype(low)
    q_enc = split(product(h_zero, enc_query).astype(low))
    k_enc = split(product(x_norm, enc_key).astype(low))
    v_enc = split(product(x_norm, enc_value).astype(low))

    def scores_of(q, k):
        return jnp.einsum("qhd,khd->hqk", q, k, preferred_element_type=jnp.float32) * HD ** (-0.5)

    p_enc = jax.nn.softmax(scores_of(q_enc, k_enc), axis=-1)
    o_enc = jnp.einsum("hqk,khd->qhd", p_enc.astype(low), v_enc, preferred_element_type=jnp.float32)
    o_enc_low = o_enc.reshape(rows, HEADS * HD).astype(low)
    z_one = z_zero + product(o_enc_low, enc_output)
    h_one = layer_norm(z_one, norm_gains[1]).astype(low)
    projected = product(h_one, self_project).astype(low).reshape(rows, n_head, 3 * width)
    projected = projected.transpose(1, 0, 2)
    q_self, kv_self = spread_rows(dims, projected[:, :, :width], projected[:, :, width:], 1)
    q_self = q_self.reshape(blk_rows, width)
    kv_self = kv_self.reshape(n_blk * blk_rows, 2 * width)
    out_self, lse_self, out_self_t = attend(bounds, q_self, kv_self, heads_here)
    o_self_low = swap_heads(dims, out_self.reshape(n_head, rows, width), 2)
    o_self_low = o_self_low.transpose(1, 0, 2).reshape(rows, HEADS * HD)
    z_two = z_one + product(o_self_low, self_output)
    h_two = layer_norm(z_two, norm_gains[2]).astype(low)
    pre_act = product(h_two, hidden_in)
    activ = jax.nn.gelu(pre_act).astype(low)
    z_three = z_two + product(activ, hidden_out)
    decoded_low = (layer_norm(z_three, norm_gains[3]) + product(out_queries, query_table)).astype(low)
    logits = product(decoded_low, class_table)
    is_target = (labels[:, None] == jnp.arange(C, dtype=jnp.int32)[None, :]).astype(jnp.float32)
    row_top = jnp.max(logits, -1, keepdims=True)
    row_lse = row_top + jnp.log(jnp.sum(jnp.exp(logits - row_top), -1, keepdims=True))
    target = jnp.sum(is_target * logits, -1, keepdims=True)
    member = (
        (modality[:, None] == jnp.arange(MODES, dtype=jnp.int32)[None, :]) & (labeled[:, None] == 1)
    ).astype(jnp.float32)
    label_counts = lax.psum(jnp.sum(member, 0), ("blk", "head"))
    loss_sums = lax.psum(jnp.sum((row_lse - target) * member, 0), ("blk", "head"))

    row_weight = jnp.sum(member / jnp.maximum(label_counts, 1.0)[None, :], 1, keepdims=True)
    dlogits = (row_weight * (jnp.exp(logits - row_lse) - is_target)).astype(low)
    class_grad = inner(decoded_low, dlogits)
    d_decoded = against(dlogits, class_table)
    query_grad = inner(out_queries, d_decoded.astype(low))
    d_three, gain_three = norm_pullback(z_three, norm_gains[3], d_decoded)
    d_branch = d_three.astype(low)
    out_grad = inner(activ, d_branch)
    unused, gelu_pull = jax.vjp(jax.nn.gelu, pre_act)
    d_pre = gelu_pull(against(d_branch, hidden_out))[0].astype(low)
    in_grad = inner(h_two, d_pre)
    d_middle, gain_two = norm_pullback(z_two, norm_gains[2], against(d_pre, hidden_in))
    d_two = d_three + d_middle
    d_branch = d_two.astype(low)
    self_out_grad = inner(o_self_low, d_branch)
    dout_self = against(d_branch, self_output).astype(low)
    dout_self = swap_heads(
        dims, dout_self.reshape(rows, n_head, width).transpose(1, 0, 2), 3
    ).reshape(blk_rows, width)
    d_q, d_kv = attend_back(bounds, q_self, kv_self, dout_self, out_self_t, lse_self, heads_here)
    d_kv = collect_rows(dims, d_kv.reshape(n_blk, blk_rows, 2 * width), 4)
    d_projected = swap_heads(
        dims, jnp.concatenate([d_q, d_kv], 1).reshape(n_head, rows, 3 * width), 5
    )
    d_projected = d_projected.transpose(1, 0, 2).reshape(rows, n_head * 3 * width)
    project_grad = inner(h_one, d_projected)
    d_middle, gain_one = norm_pullback(z_one, norm_gains[1], against(d_projected, self_project))
    d_one = d_two + d_middle
    d_branch = d_one.astype(low)
    enc_out_grad = inner(o_enc_low, d_branch)
    dout_enc = split(against(d_branch, enc_output).astype(low))
    dp_enc = jnp.einsum("qhd,khd->hqk", dout_enc, v_enc, preferred_element_type=jnp.float32)
    delta_enc = jnp.einsum("qhd,qhd->hq", dout_enc.astype(jnp.float32), o_enc)
    ds_enc = (p_enc * (dp_enc - delta_enc[..., None])).astype(low)
    d_q_enc = jnp.einsum("hqk,khd->qhd", ds_enc, k_enc, preferred_element_type=jnp.float32) * HD ** (-0.5)
    d_k_enc = jnp.einsum("hqk,qhd->khd", ds_enc, q_enc, preferred_element_type=jnp.float32) * HD ** (-0.5)
    d_v_enc = jnp.einsum(
        "hqk,qhd->khd", p_enc.astype(low), dout_enc, preferred_element_type=jnp.float32
    )
    d_q_enc, d_k_enc, d_v_enc = (x.reshape(-1, HEADS * HD).astype(low) for x in (d_q_enc, d_k_enc, d_v_enc))
    enc_query_grad = inner(h_zero, d_q_enc)
    enc_key_grad = inner(x_norm, d_k_enc)
    enc_value_grad = inner(x_norm, d_v_enc)
    d_middle, gain_zero = norm_pullback(z_zero, norm_gains[0], against(d_q_enc, enc_query))
    d_zero = d_one + d_middle
    d_zero_top = d_zero.astype(low)
    d_zero_rest = (d_zero - d_zero_top.astype(jnp.float32)).astype(low)
    latent_grad = inner(picked, d_zero_top) + inner(picked, d_zero_rest)

    def columns(whole, g):
        size = whole.shape[1] // n_head
        return whole[:, g * size : (g + 1) * size]

    def of_rows(whole, g):
        size = whole.shape[0] // n_head
        return whole[g * size : (g + 1) * size]

    flat = []
    for g in range(n_head):
        group = [
            columns(enc_query_grad, g),
            jnp.concatenate([columns(enc_key_grad, g), columns(enc_value_grad, g)], 1),
            of_rows(enc_out_grad, g),
            columns(project_grad, g),
            of_rows(self_out_grad, g),
            columns(in_grad, g),
            of_rows(out_grad, g),
            columns(class_grad, g),
        ]
        flat.append(jnp.concatenate([w.astype(low).reshape(-1) for w in group]).reshape(n_blk, n_h))
    flat = jnp.pad(jnp.stack(flat, 1), ((0, 0), (0, 0), (0, head_rows * LANES - n_h)))
    gains = jnp.stack([gain_zero, gain_one, gain_two, gain_three])
    common = jnp.concatenate([w.astype(low).reshape(-1) for w in (query_grad, latent_grad, gains)])
    common = jnp.pad(common.reshape(n_blk, n_c), ((0, 0), (0, n_head * piece_rows * LANES - n_c)))
    blocks = jnp.concatenate(
        [
            flat.reshape(n_blk, n_head, head_rows, LANES),
            common.reshape(n_blk, n_head, piece_rows, LANES),
        ],
        2,
    )
    share = reduce_all(dims, blocks, 6)
    clip_norm = jnp.sqrt(lax.psum(jnp.sum(share * share), ("blk", "head")))
    factor = jnp.minimum(1.0, clip_limit / clip_norm)
    head_share = share[:head_rows].reshape(-1)[:n_h]
    common_share = lax.all_gather(share[head_rows:].astype(low), "head", axis=0, tiled=True)
    common_share = common_share.reshape(-1)[:n_c].astype(jnp.float32)
    head_out = adam_step(head_params, head_first, head_second, head_share * factor)
    common_out = adam_step(common_params, common_first, common_second, common_share * factor)
    return head_out + common_out + (loss_sums, label_counts, clip_norm)


def solution(mesh):
    placed = (
        P("blk", None),
        P("blk", None),
        P(),
        P("blk"),
        P("blk"),
        P("blk"),
        P(("head", "blk")),
        P(("head", "blk")),
        P(("head", "blk")),
        P("blk"),
        P("blk"),
        P("blk"),
    )
    return jax.shard_map(
        per_device,
        mesh=mesh,
        in_specs=placed,
        out_specs=(
            P(("head", "blk")),
            P(("head", "blk")),
            P(("head", "blk")),
            P(("head", "blk")),
            P("blk"),
            P("blk"),
            P("blk"),
            P("blk"),
            P(),
            P(),
            P(),
        ),
        check_vma=False,
    )
```

time: 1330 us -> 892 us (0.67)
  waiting for transfers between devices: 626 us -> 0 us
  Pallas kernels: 0 us -> 411 us
  matrix products: 269 us -> 53.2 us
  local copies, waits for them, and re-layouts: 125 us -> 275 us
  other arithmetic: 163 us -> 42.5 us
  between operations: 20.4 us -> 4.79 us
    pallas_call x0 -> x9, Pallas kernels: none -> 411 us  [the longest x1 72.6 us: reduce_all(): pl.pallas_call(functools.partial(reduce_kernel, dims, parts, row_chunk),...]
    dot_general x62 -> x5, matrix products: 228 us -> 8.13 us  [the longest x1 3.27 us: per_device(): jnp.einsum('qhd,khd->hqk', dout_enc, v_enc, preferred_element_type=jnp.fl...]
    psum x7 -> x0, waiting for transfers between devices: 182 us -> none  [over_heads(): return lax.psum(x.astype(jnp.bfloat16), 'head').astype(jnp.float32)]
    all_gather x4 -> x0, waiting for transfers between devices: 165 us -> none  [the longest x1 67.6 us: per_device(): lax.all_gather(common_params.astype(jnp.bfloat16), 'blk', axis=0, tiled=T...]
    unnamed x15 -> x0, waiting for transfers between devices: 157 us -> none
    reduce_scatter x2 -> x0, waiting for transfers between devices: 122 us -> none  [the longest x1 71.1 us: per_device(): lax.psum_scatter(key_parts[0].reshape(amount_all, width).astype(jnp.bfloa...]
    slice x21 -> x55, local copies, waits for them, and re-layouts: 23.6 us -> 130 us  [the longest x32 96 us: per_device(): flat[border:border + amount].reshape(shape)]
    reduce_sum x31 -> x5, other arithmetic: 47.9 us -> 3.54 us  [the longest x1 1.9 us: per_device(): clip_norm = jnp.sqrt(lax.psum(jnp.sum(share * share), ('blk', 'head')))]
  transfers between devices with their start and end apart: 14 -> 0, of which waited for: 13 -> 0; matrix products, arithmetic and copies ran while one was open for 9% -> 0% of each run, Pallas kernels for 0% -> 0%
where the time goes in v1:
time: 892 us; the launch traced here: 881 us
  Pallas kernels  411 us (46%)
  local copies, waits for them, and re-layouts  275 us (31%)
  blocking collectives  94.8 us (11%)
  matrix products  53.2 us (6%)
  other arithmetic  42.5 us (5%)
    slice x32, local copies, waits for them, and re-layouts, per_device(): flat[border:border + amount].reshape(shape)  96 us
    pallas_call x1, Pallas kernels, reduce_all(): pl.pallas_call(functools.partial(reduce_kernel, dims, parts, row_chunk),...  72.6 us
    pallas_call x1, Pallas kernels, collect_rows(): pl.pallas_call(functools.partial(collect_kernel, dims), out_shape=jax.Sha...  72.4 us
    pallas_call x1, Pallas kernels, spread_rows(): pl.pallas_call(functools.partial(spread_kernel, dims), out_shape=(jax.Sha...  71.3 us
    unnamed x348, local copies, waits for them, and re-layouts  69.2 us
    pallas_call x1, Pallas kernels, gather_all(): pl.pallas_call(functools.partial(gather_kernel, dims, parts), out_shape=j...  62.2 us
    pallas_call x1, Pallas kernels, attend_back(): pl.pallas_call(functools.partial(attend_back_kernel, heads, key_step), ou...  55.6 us
    pallas_call x1, Pallas kernels, attend(): pl.pallas_call(functools.partial(attend_kernel, heads, key_step, query_st...  53.8 us

profile of v1, /device:TPU:0, one launch (start us, length us, event | category | flops | bytes accessed | tf_op | source)
XLA Modules:
  0.0 881.3 jit_solution(10613428313707733183)
XLA Ops:
  6.5 42.0 %psum.21 = f32[3]{0:T(128)S(1)} all-reduce(f32[3]{0:T(128)S(1)} %get-tuple-element.55), channel_id=1, replica_groups=mesh['blk'=8,'head'=4] {'blk','head'}, use_global_device_ids=true, to_apply=%region_9.10 | all-reduce | flops 3 | bytes 24 | tf_op jit(solution)/shard_map/psum | solution.py:872
  54.3 62.2 %gather_weights.1 = bf16[8,4,1408,128]{3,2,1,0:T(8,128)(2,1)} custom-call(bf16[1408,128]{1,0:T(8,128)(2,1)} %pad_maximum_fusion.9.src), custom_call_target="tpu_custom_call" | custom-call | tf_op jit(solution)/shard_map/gather_weights/pallas_call | solution.py:178
  116.5 5.9 slice_bitcast_fusion.3
  125.0 7.1 copy_bitcast_fusion.3
  132.1 5.5 slice.394
  146.6 6.6 slice.428
  154.9 2.3 fusion.120
  157.2 4.2 slice.416
  162.9 6.6 slice.404
  171.3 3.0 fusion.115
  181.1 6.6 slice.426
  191.7 4.1 slice.414
  197.4 6.6 slice.400
  205.7 8.3 copy_bitcast_fusion.1
  219.2 6.6 slice.432
  227.5 2.3 fusion.122
  229.8 4.2 slice.420
  235.5 6.6 slice.412
  243.9 3.0 fusion.117
  253.6 6.6 slice.430
  261.9 2.3 fusion.121
  264.2 4.1 slice.418
  269.9 6.7 slice.408
  277.7 2.6 convolution_convert_fusion.12
  282.4 4.8 fusion.137
  287.8 2.6 fusion.22
  300.2 71.3 %spread_rows.1 = (bf16[4,256,128]{2,1,0:T(8,128)(2,1)}, bf16[8,4,256,256]{3,2,1,0:T(8,128)(2,1)}) custom-call(bf16[4,256,128]{2,1,0:T(8,128)(2,1)} %slice.528.q_in, bf16[4,256,256]{2,1,0:T(8,128)(2,1)} %slice.529.kv_in), custom_call_target="tpu_custom_call" | custom-call | tf_op jit(solution)/shard_map/spread_rows/pallas_call | solution.py:390
  371.6 53.8 %attend.1 = (bf16[1024,128]{1,0:T(8,128)(2,1)}, f32[2,1024]{1,0:T(2,128)}, f32[128,1024]{1,0:T(8,128)}) custom-call(s32[2,6]{1,0:T(2,128)} %pad_add_fusion.bounds, bf16[1024,128]{1,0:T(8,128)(2,1)} %bitcast.266, bf16[8192,256]{1,0:T(8,128)(2,1)} %bitcast.232), custom_call_target="tpu_custom_call" | custom-call | tf_op jit(solution)/shard_map/attend/pallas_call | solution.py:633
  425.4 5.7 swap_heads.3
  442.4 5.8 fusion.18
  456.4 5.7 swap_heads.4
  462.1 55.6 %attend_back.1 = (bf16[1024,128]{1,0:T(8,128)(2,1)}, bf16[8192,256]{1,0:T(8,128)(2,1)}) custom-call(s32[2,6]{1,0:T(2,128)} %pad_add_fusion.bounds, bf16[1024,128]{1,0:T(8,128)(2,1)} %bitcast.267, bf16[8192,256]{1,0:T(8,128)(2,1)} %bitcast.233, bf16[1024,128]{1,0:T(8,128)(2,1)} %bitcast.270, f32[128,1024]{1,0:T(8,128)} %get-tuple-element.21.out_t, ...), custom_call_target="tpu_custom_call" | custom-call | tf_op jit(solution)/shard_map/attend_back/pallas_call | solution.py:699
  519.9 72.4 %collect_rows.1 = bf16[1024,256]{1,0:T(8,128)(2,1)S(1)} custom-call(bf16[8,1024,256]{2,1,0:T(8,128)(2,1)S(1)} %bitcast.230), custom_call_target="tpu_custom_call" | custom-call | tf_op jit(solution)/shard_map/collect_rows/pallas_call | solution.py:507
  593.3 11.4 %swap_heads.5 = bf16[4,256,384]{2,1,0:T(8,128)(2,1)} custom-call(bf16[4,256,384]{2,1,0:T(8,128)(2,1)} %bitcast.247), custom_call_target="tpu_custom_call" | custom-call | tf_op jit(solution)/shard_map/swap_heads/pallas_call | solution.py:433
  606.2 3.0 multiply_reduce_fusion.7
  614.5 3.3 multiply_convert_fusion
  673.4 2.8 reshape.560
  680.0 4.7 reshape.566
  694.2 4.2 stack_reshape.12
  705.6 4.2 stack_reshape.15
  717.1 4.2 stack_reshape.14
  727.4 4.1 stack_reshape.13
  731.5 6.9 fusion.8
  738.4 8.0 pad_maximum_fusion.src
  746.5 72.6 %reduce_gradients.1 = f32[1408,128]{1,0:T(8,128)} custom-call(bf16[8,4,1408,128]{3,2,1,0:T(8,128)(2,1)} %pad_maximum_fusion.src), custom_call_target="tpu_custom_call" | custom-call | tf_op jit(solution)/shard_map/reduce_gradients/pallas_call | solution.py:303
  821.0 46.2 %all-reduce.4 = (f32[]{:T(128)}, f32[3]{0:T(128)}) all-reduce(f32[]{:T(128)} %multiply_reduce_fusion.1, f32[3]{0:T(128)S(1)} %copy-done.140), channel_id=1, replica_groups=mesh['blk'=8,'head'=4] {'blk','head'}, use_global_device_ids=true, to_apply=%region_32.33 | all-reduce | flops 4 | bytes 32 | tf_op jit(solution)/shard_map/psum | solution.py:957
  868.9 6.6 all_gather.3
  875.5 2.8 fusion.106
  (510 shorter events, 197.7 us)
Async XLA Ops:
  0.6 436.3 %copy-start = (bf16[1024,1026]{0,1:T(8,128)(2,1)S(1)}, bf16[1024,1026]{0,1:T(8,128)(2,1)}, u32[]{:S(2)}) copy-start(bf16[1024,1026]{0,1:T(8,128)(2,1)} %param.13) | copy-start | bytes 6303748
  0.7 52.8 %copy-start.18 = (f32[148480]{0:T(1024)S(1)}, f32[148480]{0:T(1024)}, u32[]{:S(2)}) copy-start(f32[148480]{0:T(1024)} %param.18) | copy-start | bytes 1781764
  49.1 90.0 %copy-start.118 = (s32[256]{0:T(256)}, s32[256]{0:T(256)S(1)}, u32[]{:S(2)}) copy-start(s32[256]{0:T(256)S(1)} %and_select_fusion) | copy-start | bytes 3076
  50.4 66.1 %copy-start.130 = (f32[512]{0:T(512)}, f32[512]{0:T(512)S(1)}, u32[]{:S(2)}) copy-start(f32[512]{0:T(512)S(1)} %broadcast_multiply_fusion) | copy-start | bytes 6148
  116.5 5.9 slice-start
  140.8 151.2 %copy-start.6 = (f32[256,512]{1,0:T(8,128)}, f32[256,512]{1,0:T(8,128)S(1)}, u32[]{:S(2)}) copy-start(f32[256,512]{1,0:T(8,128)S(1)} %get-tuple-element.136) | copy-start | bytes 1572868
  269.9 7.7 copy-start.77
  269.9 7.7 copy-start.79
  269.9 7.7 copy-start.81
  269.9 7.8 copy-start.131
  269.9 7.8 copy-start.135
  282.4 4.8 copy-start.46
  425.4 8.8 copy-start.58
  433.9 19.9 %copy-start.8 = (f32[256,512]{1,0:T(8,128)}, f32[256,512]{1,0:T(8,128)S(1)}, u32[]{:S(2)}) copy-start(f32[256,512]{1,0:T(8,128)S(1)} %get-tuple-element.144) | copy-start | bytes 1572868
  433.9 19.9 %copy-start.113 = (f32[256]{0:T(256)}, f32[256]{0:T(256)S(1)}, u32[]{:S(2)}) copy-start(f32[256]{0:T(256)S(1)} %broadcast_multiply_fusion.2) | copy-start | bytes 3076
  434.2 19.6 %copy-start.122 = (f32[256]{0:T(256)}, f32[256]{0:T(256)S(1)}, u32[]{:S(2)}) copy-start(f32[256]{0:T(256)S(1)} %fusion.84) | copy-start | bytes 3076
  519.9 72.4 %copy-start.75 = (bf16[1024,128]{1,0:T(8,128)(2,1)S(1)}, bf16[1024,128]{1,0:T(8,128)(2,1)}, u32[]{:S(2)}) copy-start(bf16[1024,128]{1,0:T(8,128)(2,1)} %get-tuple-element.23) | copy-start | bytes 786436
  630.4 4.4 copy-start.68
  630.4 4.4 copy-start.132
  630.4 4.4 copy-start.136
  648.6 13.6 %copy-start.9 = (f32[256,512]{1,0:T(8,128)S(1)}, f32[256,512]{1,0:T(8,128)}, u32[]{:S(2)}) copy-start(f32[256,512]{1,0:T(8,128)} %copy-done.8) | copy-start | bytes 1572868
  664.7 5.1 copy-start.33
  665.7 5.1 copy-start.32
  666.7 5.3 copy-start.21
  670.8 5.4 copy-start.12
  688.0 4.6 copy-start.22
  688.0 5.5 copy-start.48
  694.2 7.6 copy-start.39
  694.2 8.3 copy-start.56
  694.2 9.0 %copy-start.28 = (bf16[64,4,8,128]{3,1,2,0:T(4,128)(2,1)S(1)}, bf16[64,4,8,128]{3,1,2,0:T(4,128)(2,1)}, u32[]{:S(2)}) copy-start(bf16[64,4,8,128]{3,1,2,0:T(4,128)(2,1)} %copy.90) | copy-start | bytes 1572868
  698.4 5.7 copy-start.29
  698.4 6.5 copy-start.51
  705.6 7.6 copy-start.37
  705.6 8.4 copy-start.55
  705.6 9.1 %copy-start.26 = (bf16[64,4,8,128]{3,1,2,0:T(4,128)(2,1)S(1)}, bf16[64,4,8,128]{3,1,2,0:T(4,128)(2,1)}, u32[]{:S(2)}) copy-start(bf16[64,4,8,128]{3,1,2,0:T(4,128)(2,1)} %copy.85) | copy-start | bytes 1572868
  709.9 5.6 copy-start.27
  709.9 6.5 copy-start.50
  717.1 7.3 copy-start.53
  717.1 8.0 copy-start.24
  721.3 4.6 copy-start.25
  721.3 5.4 copy-start.49
  731.5 6.9 copy-start.5
  746.5 74.6 %copy-start.140 = (f32[3]{0:T(128)S(1)}, f32[3]{0:T(128)}, u32[]{:S(2)}) copy-start(f32[3]{0:T(128)} %get-tuple-element.35) | copy-start | bytes 40
  746.5 129.0 %copy-start.19 = (f32[148480]{0:T(1024)S(1)}, f32[148480]{0:T(1024)}, u32[]{:S(2)}) copy-start(f32[148480]{0:T(1024)} %param.18) | copy-start | bytes 1781764
  746.5 129.0 %copy-start.52 = (f32[148480]{0:T(1024)S(1)}, f32[148480]{0:T(1024)}, u32[]{:S(2)}) copy-start(f32[148480]{0:T(1024)} %param.19) | copy-start | bytes 1781764
  868.9 9.5 %copy-start.36 = (f32[116096]{0:T(1024)S(1)}, f32[116096]{0:T(1024)}, u32[]{:S(2)}) copy-start(f32[116096]{0:T(1024)} %param.21) | copy-start | bytes 1393156
  868.9 9.5 %copy-start.69 = (f32[116096]{0:T(1024)S(1)}, f32[116096]{0:T(1024)}, u32[]{:S(2)}) copy-start(f32[116096]{0:T(1024)} %param.22) | copy-start | bytes 1393156
  868.9 9.4 %copy-start.70 = (f32[116096]{0:T(1024)S(1)}, f32[116096]{0:T(1024)}, u32[]{:S(2)}) copy-start(f32[116096]{0:T(1024)} %param.23) | copy-start | bytes 1393156
  (96 other events, 208.6 us)

commit v2 on v1

--- a/solution.py
+++ b/solution.py
@@ -102,7 +102,7 @@
 def gather_plan(dims, parts):
     plan = []
     for position in range(4):
-        for p, (first, rows, order) in enumerate(parts):
+        for p, (array, first, rows, order) in enumerate(parts):
             axis = order[position]
             done = order[:position]
             offsets = [(0, 0, 0, 0)]
@@ -118,24 +118,24 @@
     return plan
 
 
-def gather_kernel(dims, parts, src, out, send_sem, recv_sem, own_sem):
+def gather_kernel(dims, parts, count, *refs):
+    srcs, outs = refs[:count], refs[count : 2 * count]
+    send_sem, recv_sem, own_sem = refs[2 * count :]
     me = my_place(dims)
     plan = gather_plan(dims, parts)
     number = {(p, offset): i for i, (p, offset, position) in enumerate(plan)}
     axes = [a for a in range(4) if dims[a] > 1]
     greet(dims, me, axis_peers(dims, axes))
-    own = pltpu.make_async_copy(src, out.at[blk_of(dims, me), head_of(dims, me)], own_sem)
-    own.start()
     started = []
 
     def block(p, offset):
         place = shifted(dims, me, offset, -1)
-        first, rows, order = parts[p]
-        return out.at[blk_of(dims, place), head_of(dims, place), pl.ds(first, rows)]
+        array, first, rows, order = parts[p]
+        return outs[array].at[blk_of(dims, place), head_of(dims, place), pl.ds(first, rows)]
 
     def forward(p, offset, position):
-        first, rows, order = parts[p]
-        source = src.at[pl.ds(first, rows)] if position < 0 else block(p, offset)
+        array, first, rows, order = parts[p]
+        source = srcs[array].at[pl.ds(first, rows)] if position < 0 else block(p, offset)
         for axis in order[position + 1 :]:
             for d in range(1, dims[axis]):
                 i = number[(p, tuple(d if a == axis else offset[a] for a in range(4)))]
@@ -152,9 +152,16 @@
 
     for p in range(len(parts)):
         forward(p, (0, 0, 0, 0), -1)
+    own = []
+    for array in range(count):
+        copy = pltpu.make_async_copy(
+            srcs[array], outs[array].at[blk_of(dims, me), head_of(dims, me)], own_sem.at[array]
+        )
+        copy.start()
+        own.append(copy)
     for i, (p, offset, position) in enumerate(plan):
         landed = block(p, offset)
-        axis = parts[p][2][position]
+        axis = parts[p][3][position]
         remote(
             landed,
             landed,
@@ -166,28 +173,37 @@
         forward(p, offset, position)
     for copy in started:
         copy.wait_send()
-    own.wait()
-
-
-def gather_all(dims, shard, collective_id):
-    rows = shard.shape[0]
+    for copy in own:
+        copy.wait()
+
+
+def halves(array, rows, orders):
     first = rows // 2 // TILE * TILE
-    parts = ((0, first, (0, 1, 2, 3)), (first, rows - first, (0, 2, 1, 3)))
+    return ((array, 0, first, orders[0]), (array, first, rows - first, orders[1]))
+
+
+def gather_all(dims, shards, collective_id):
+    parts = halves(0, shards[0].shape[0], ((0, 1, 2, 3), (0, 2, 1, 3))) + (
+        (1, 0, shards[1].shape[0], (0, 2, 1, 3)),
+    )
     count = len(gather_plan(dims, parts))
     z, y, x, cores = dims
+    any_space = pl.BlockSpec(memory_space=pl.ANY)
     return pl.pallas_call(
-        functools.partial(gather_kernel, dims, parts),
-        out_shape=jax.ShapeDtypeStruct((z * y, x * cores) + shard.shape, shard.dtype),
-        in_specs=[pl.BlockSpec(memory_space=pl.ANY)],
-        out_specs=pl.BlockSpec(memory_space=pl.ANY),
+        functools.partial(gather_kernel, dims, parts, len(shards)),
+        out_shape=[
+            jax.ShapeDtypeStruct((z * y, x * cores) + shard.shape, shard.dtype) for shard in shards
+        ],
+        in_specs=[any_space] * len(shards),
+        out_specs=[any_space] * len(shards),
         scratch_shapes=[
             pltpu.SemaphoreType.DMA((count,)),
             pltpu.SemaphoreType.DMA((count,)),
-            pltpu.SemaphoreType.DMA(()),
+            pltpu.SemaphoreType.DMA((len(shards),)),
         ],
         compiler_params=pltpu.CompilerParams(collective_id=collective_id, has_side_effects=True),
         name="gather_weights",
-    )(shard)
+    )(*shards)
 
 
 def reduce_plan(dims, order):
@@ -205,45 +221,49 @@
     return stages
 
 
-def reduce_kernel(dims, parts, chunk, src, out, *scratch):
+def reduce_kernel(dims, parts, chunk, valid, *refs):
+    count = len(valid)
+    srcs, tile = refs[:count], refs[count]
+    outs, totals, shares = refs[count + 1 : 2 * count + 1], refs[2 * count + 1], refs[2 * count + 2]
+    scratch = refs[2 * count + 3 :]
     me = my_place(dims)
+    z, y, x, cores = dims
     places = len(parts) * 4
-    buffers, send_sem, recv_sem = scratch[:places], scratch[places], scratch[places + 1]
+    buffers = scratch[:places]
+    send_sem, recv_sem, near_tiles, far_tiles = scratch[places : places + 4]
     axes = [a for a in range(4) if dims[a] > 1]
-    greet(dims, me, axis_peers(dims, axes))
+    across = [(0, 0, a, c) for a in range(x) for c in range(cores) if (a, c) != (0, 0)]
+    others = [(a, b, 0, 0) for a in range(z) for b in range(y) if (a, b) != (0, 0)]
+    greet(dims, me, axis_peers(dims, axes) + [o for o in across + others if sum(v != 0 for v in o) > 1])
     started = []
-    numbers = [0]
     pending = {}
 
+    def push(src, dst, offset):
+        i = len(started)
+        copy = remote(src, dst, send_sem.at[i], recv_sem.at[i], shifted(dims, me, offset, 1), dims)
+        copy.start()
+        started.append(copy)
+        return copy
+
+    stages = [reduce_plan(dims, part[3]) for part in parts]
+
     def source(p, position, offset):
-        first, rows, order = parts[p]
+        array, first, rows, order = parts[p]
         if position == 0:
             place = shifted(dims, me, offset, 1)
-            return src.at[blk_of(dims, place), head_of(dims, place), pl.ds(first, rows)]
+            return srcs[array].at[blk_of(dims, place), head_of(dims, place), pl.ds(first, rows)]
         k = stages[p][position - 1][1].index(offset)
         return buffers[p * 4 + position - 1].at[k, 0]
 
-    stages = [reduce_plan(dims, order) for first, rows, order in parts]
-
     def send(p, position, k, d):
         axis, offsets = stages[p][position]
-        i = numbers[0]
-        numbers[0] += 1
         there = tuple(d if a == axis else offsets[k][a] for a in range(4))
-        copy = remote(
-            source(p, position, there),
-            buffers[p * 4 + position].at[k, d - 1],
-            send_sem.at[i],
-            recv_sem.at[i],
-            shifted(dims, me, along(axis, d), 1),
-            dims,
+        pending[(p, position, k, d)] = push(
+            source(p, position, there), buffers[p * 4 + position].at[k, d - 1], along(axis, d)
         )
-        copy.start()
-        started.append(copy)
-        pending[(p, position, k, d)] = copy
 
     def add(p, position, k):
-        first, rows, order = parts[p]
+        array, first, rows, order = parts[p]
         axis, offsets = stages[p][position]
         for d in range(1, dims[axis]):
             pending[(p, position, k, d)].wait_recv()
@@ -259,16 +279,15 @@
             for d in range(1, dims[axis]):
                 total = total + arrived[k, d - 1, at].astype(jnp.float32)
             if last:
-                out[pl.ds(pl.multiple_of(first + n * step, TILE), step)] = total
+                outs[array][pl.ds(pl.multiple_of(first + n * step, TILE), step)] = total
             else:
                 arrived[k, 0, at] = total.astype(low)
 
+    for k in range(len(stages[0][0][1])):
+        for p in range(len(parts)):
+            for d in range(1, dims[stages[p][0][0]]):
+                send(p, 0, k, d)
     for position in range(4):
-        for k in range(len(stages[0][position][1])):
-            for p in range(len(parts)):
-                if position == 0:
-                    for d in range(1, dims[stages[p][0][0]]):
-                        send(p, 0, k, d)
         for k in range(len(stages[0][position][1])):
             for p in range(len(parts)):
                 add(p, position, k)
@@ -278,6 +297,26 @@
                     rest = tuple(0 if a == axis else offset[a] for a in range(4))
                     if offset[axis]:
                         send(p, position + 1, offsets.index(rest), offset[axis])
+    my_head, my_blk = head_of(dims, me), blk_of(dims, me)
+    shares[my_head] = outs[count - 1][...].astype(low)
+    share_copies = [push(shares.at[my_head], shares.at[my_head], o) for o in across]
+    squares = jnp.zeros((1, LANES), jnp.float32)
+    for out, amount in zip(outs, valid):
+        squares = squares + jnp.sum(out[:amount] * out[:amount], 0, keepdims=True)
+    lane = lax.broadcasted_iota(jnp.int32, (1, LANES), 1)
+    near_tiles[my_head] = tile[...] + jnp.where(
+        lane == MODES, jnp.sum(squares, 1, keepdims=True), 0.0
+    )
+    near = [push(near_tiles.at[my_head], near_tiles.at[my_head], o) for o in across]
+    for copy in near:
+        copy.wait_recv()
+    far_tiles[my_blk] = jnp.sum(near_tiles[...], 0)
+    far = [push(far_tiles.at[my_blk], far_tiles.at[my_blk], o) for o in others]
+    for copy in far:
+        copy.wait_recv()
+    totals[...] = jnp.sum(far_tiles[...], 0)
+    for copy in share_copies:
+        copy.wait_recv()
     for copy in started:
         copy.wait_send()
 
@@ -289,29 +328,41 @@
     return rows
 
 
-def reduce_all(dims, blocks, collective_id):
-    rows = blocks.shape[2]
-    first = rows // 2 // TILE * TILE
-    parts = ((0, first, (3, 2, 1, 0)), (first, rows - first, (3, 1, 2, 0)))
+def reduce_all(dims, arrays, valid, tile, collective_id):
+    z, y, x, cores = dims
+    parts = halves(0, arrays[0].shape[2], ((3, 2, 1, 0), (3, 1, 2, 0))) + (
+        (1, 0, arrays[1].shape[2], (3, 1, 2, 0)),
+    )
     scratch = []
-    count = 0
-    for start, amount, order in parts:
+    count = 2 * (x * cores - 1) + z * y - 1
+    for array, start, amount, order in parts:
         for axis, offsets in reduce_plan(dims, order):
             others = max(dims[axis] - 1, 1)
             count += len(offsets) * (dims[axis] - 1)
             scratch.append(pltpu.VMEM((len(offsets), others, amount, LANES), low))
+    vmem = pl.BlockSpec(memory_space=pltpu.VMEM)
+    last_rows = arrays[-1].shape[2]
     return pl.pallas_call(
-        functools.partial(reduce_kernel, dims, parts, row_chunk),
-        out_shape=jax.ShapeDtypeStruct((rows, LANES), jnp.float32),
-        in_specs=[pl.BlockSpec(memory_space=pltpu.VMEM)],
-        out_specs=pl.BlockSpec(memory_space=pltpu.VMEM),
+        functools.partial(reduce_kernel, dims, parts, row_chunk, valid),
+        out_shape=[jax.ShapeDtypeStruct(array.shape[2:], jnp.float32) for array in arrays]
+        + [
+            jax.ShapeDtypeStruct((8, LANES), jnp.float32),
+            jax.ShapeDtypeStruct((x * cores, last_rows, LANES), low),
+        ],
+        in_specs=[vmem] * (len(arrays) + 1),
+        out_specs=[vmem] * (len(arrays) + 2),
         scratch_shapes=scratch
-        + [pltpu.SemaphoreType.DMA((count,)), pltpu.SemaphoreType.DMA((count,))],
+        + [
+            pltpu.SemaphoreType.DMA((count,)),
+            pltpu.SemaphoreType.DMA((count,)),
+            pltpu.VMEM((x * cores, 8, LANES), jnp.float32),
+            pltpu.VMEM((z * y, 8, LANES), jnp.float32),
+        ],
         compiler_params=pltpu.CompilerParams(
             collective_id=collective_id, has_side_effects=True, vmem_limit_bytes=56 * MIB
         ),
         name="reduce_gradients",
-    )(blocks)
+    )(*arrays, tile)
 
 
 def spread_kernel(dims, q_in, kv_in, q_out, kv_out, send_sem, recv_sem, own_sem):
@@ -718,34 +769,591 @@
     )(bounds, q, kv, dout, out_t, lse)
 
 
-def layer_norm(x, gain):
-    centre = x - jnp.mean(x, -1, keepdims=True)
-    return centre * lax.rsqrt(jnp.mean(centre * centre, -1, keepdims=True) + norm_eps) * gain
-
-
-def norm_pullback(x, gain, grad):
-    unused, pull = jax.vjp(layer_norm, x, gain)
-    return pull(grad)
-
-
-def inner(a, b):
-    return lax.dot_general(a, b, (((0,), (0,)), ((), ())), preferred_element_type=jnp.float32)
-
-
 def part_shapes(n_head):
     width = HEADS // n_head * HD
     hidden = FF // n_head
-    classes = C // n_head
     return (
-        (D, width),
-        (DI, 2 * width),
-        (width, D),
-        (D, 3 * width),
-        (width, D),
-        (D, hidden),
-        (hidden, D),
-        (D, classes),
-    )
+        (D, width, True),
+        (DI, 2 * width, True),
+        (width, D, False),
+        (D, 3 * width, True),
+        (width, D, False),
+        (D, hidden, True),
+        (hidden, D, False),
+        (D, C // n_head, True),
+    )
+
+
+def borders(n_head):
+    result = [0]
+    for rows, columns, joined in part_shapes(n_head):
+        result.append(result[-1] + rows * columns // LANES)
+    return result
+
+
+def period(columns):
+    amount = 1
+    while amount * columns % LANES:
+        amount *= 2
+    return amount
+
+
+def segments(start, amount, unit):
+    result = []
+    while amount > 0:
+        which, at = divmod(start, unit)
+        size = min(unit - at, amount)
+        result.append((which, at, at + size))
+        start, amount = start + size, amount - size
+    return result
+
+
+def joined_lanes(pieces):
+    return pieces[0] if len(pieces) == 1 else jnp.concatenate(pieces, 1)
+
+
+def lane_blocks(value):
+    rows, columns = value.shape
+    missing = -columns % LANES
+    if missing:
+        value = jnp.concatenate([value, jnp.zeros((rows, missing), value.dtype)], 1)
+    return [value[:, i : i + LANES] for i in range(0, columns + missing, LANES)]
+
+
+def every(first, amount, stride):
+    return pl.ds(first, amount) if stride == 1 else pl.ds(first, amount, stride=stride)
+
+
+def matrix_of(stage, first, rows, columns, line):
+    if columns % LANES == 0:
+        stride = columns // LANES
+        for j in range(stride):
+            yield j * LANES, stage[every(first + j, rows, stride), :]
+        return
+    height = period(columns)
+    stride = height * columns // LANES
+    for k in range(height):
+        pieces = [
+            stage[every(first + which, rows // height, stride), :][:, begin:end]
+            for which, begin, end in segments(k * columns, columns, LANES)
+        ]
+        for i, piece in enumerate(lane_blocks(joined_lanes(pieces))):
+            line[i, every(k, rows // height, height), :] = piece
+    for i in range(-(-columns // LANES)):
+        yield i * LANES, line[i, :rows, : min(columns - i * LANES, LANES)]
+
+
+def matrix_into(stage, first, value, line):
+    rows, columns = value.shape
+    if columns % LANES == 0:
+        stride = columns // LANES
+        for j in range(stride):
+            stage[every(first + j, rows, stride), :] = value[:, j * LANES : (j + 1) * LANES]
+        return
+    height = period(columns)
+    stride = height * columns // LANES
+    for i, piece in enumerate(lane_blocks(value)):
+        line[i, :rows, :] = piece
+    for i in range(stride):
+        pieces = [
+            line[which, every(k, rows // height, height), :][:, begin:end]
+            for k, first_lane, last_lane in segments(i * LANES, LANES, columns)
+            for which, begin, end in segments(first_lane, last_lane - first_lane, LANES)
+        ]
+        stage[every(first + i, rows // height, stride), :] = joined_lanes(pieces)
+
+
+def load_stage(stage, held, first_shard, shard_rows, group):
+    for b in range(held.shape[0]):
+        stage[pl.ds(b * shard_rows, shard_rows), :] = held[b, group, :shard_rows, :].astype(jnp.float32)
+
+
+def load_matrices(stage, first_row, n_head, group, which, targets, line):
+    starts, shapes = borders(n_head), part_shapes(n_head)
+    for m, target in zip(which, targets):
+        rows, columns, joined = shapes[m]
+        row = 0 if joined else group * rows
+        column = group * columns if joined else 0
+        for j, value in matrix_of(stage, starts[m] - first_row, rows, columns, line):
+            size = value.shape[1]
+            target[row : row + rows, column + j : column + j + size] = value.astype(target.dtype)
+
+
+def normalized(x):
+    centre = x - jnp.mean(x, -1, keepdims=True)
+    rate = lax.rsqrt(jnp.mean(centre * centre, -1, keepdims=True) + norm_eps)
+    return centre * rate, rate
+
+
+def layer_norm(x, gain):
+    return normalized(x)[0] * gain
+
+
+def norm_pullback(x, gain, grad):
+    unit, rate = normalized(x)
+    inside = grad * gain
+    both = jnp.mean(inside * unit, -1, keepdims=True)
+    d_x = rate * (inside - jnp.mean(inside, -1, keepdims=True) - unit * both)
+    return d_x, jnp.sum(grad * unit, 0, keepdims=True)
+
+
+def head_lanes(group, heads, value):
+    width = heads * HD
+    block = value[:, group * width : (group + 1) * width]
+    lane = lax.broadcasted_iota(jnp.int32, (1, width), 1)
+    result = []
+    for a in range(heads):
+        here = (lane >= a * HD) & (lane < (a + 1) * HD)
+        result.append((here, jnp.where(here, block, jnp.zeros_like(block))))
+    return result
+
+
+def place_of(bounds, first, amount):
+    row = first + lax.broadcasted_iota(jnp.int32, (amount, 1), 0)
+    opening = jnp.zeros((amount, 1), jnp.int32)
+    for clip in range(bounds.shape[1]):
+        begin, end = bounds[0, clip], bounds[1, clip]
+        opening = jnp.where((row >= begin) & (row < end), begin, opening)
+    offset = row - opening
+    turns = jnp.floor((offset.astype(jnp.float32) + 0.5) * (1.0 / LAT)).astype(jnp.int32)
+    return offset - turns * LAT
+
+
+def picked_rows(bounds, rows, n_head):
+    first = lax.axis_index("blk") * (rows * n_head) + lax.axis_index("head") * rows
+    lane = lax.broadcasted_iota(jnp.int32, (rows, LAT), 1)
+    return jnp.where(lane == place_of(bounds, first, rows), 1.0, 0.0).astype(low)
+
+
+def enc_scores(q_head, keys):
+    return against(q_head, keys) * HD ** (-0.5)
+
+
+def encode_kernel(
+    n_head,
+    shard_rows,
+    rows,
+    bounds,
+    weights,
+    common,
+    inputs,
+    enc_query,
+    enc_keyval,
+    enc_output,
+    self_project,
+    gains,
+    z_zero,
+    h_zero,
+    x_norm,
+    q_enc,
+    kv_enc,
+    o_enc,
+    z_one,
+    h_one,
+    q_self,
+    kv_self,
+    held,
+    held_common,
+    stage,
+    stage_common,
+    line,
+    latent_table,
+    sems,
+):
+    heads = HEADS // n_head
+    width = heads * HD
+    shards = held.shape[0]
+    from_row = DQ * D // LANES // TILE * TILE
+    copies = [
+        pltpu.make_async_copy(common.at[pl.ds(from_row, held_common.shape[0])], held_common, sems.at[0]),
+        pltpu.make_async_copy(weights.at[pl.ds(0, shards)], held, sems.at[1]),
+    ]
+    for copy in copies:
+        copy.start()
+    x_norm[...] = normalized(inputs[...].astype(jnp.float32))[0].astype(low)
+    copies[0].wait()
+    stage_common[...] = held_common[...].astype(jnp.float32)
+    first = DQ * D // LANES - from_row
+    for j, value in matrix_of(stage_common, first, LAT, D, line):
+        latent_table[:, j : j + LANES] = value.astype(low)
+    for j, value in matrix_of(stage_common, first + LAT * D // LANES, 4, D, line):
+        gains[:, j : j + LANES] = value
+    picked = picked_rows(bounds, rows, n_head)
+    z_zero[...] = product(picked, latent_table[...])
+    h_zero[...] = layer_norm(z_zero[...], gains[0:1, :]).astype(low)
+    copies[1].wait()
+    for g in range(n_head):
+        load_stage(stage, held, 0, shard_rows, g)
+        load_matrices(
+            stage, 0, n_head, g, (0, 1, 2, 3), (enc_query, enc_keyval, enc_output, self_project), line
+        )
+    q_enc[...] = product(h_zero[...], enc_query[...]).astype(low)
+    kv_enc[...] = product(x_norm[...], enc_keyval[...]).astype(low)
+    for g in range(n_head):
+        keys = kv_enc[:, 2 * g * width : (2 * g + 1) * width]
+        values = kv_enc[:, (2 * g + 1) * width : (2 * g + 2) * width]
+        outcome = jnp.zeros((rows, width), jnp.float32)
+        for here, q_head in head_lanes(g, heads, q_enc[...]):
+            scores = enc_scores(q_head, keys)
+            probs = jnp.exp(scores - jnp.max(scores, 1, keepdims=True))
+            total = jnp.sum(probs, 1, keepdims=True)
+            outcome = jnp.where(here, product(probs.astype(low), values) / total, outcome)
+        o_enc[:, g * width : (g + 1) * width] = outcome.astype(low)
+    z_one[...] = z_zero[...] + product(o_enc[...], enc_output[...])
+    h_one[...] = layer_norm(z_one[...], gains[1:2, :]).astype(low)
+    projected = product(h_one[...], self_project[...]).astype(low)
+    for g in range(n_head):
+        q_self[g] = projected[:, 3 * g * width : (3 * g + 1) * width]
+        kv_self[g] = projected[:, (3 * g + 1) * width : (3 * g + 3) * width]
+
+
+VMEM_SPEC = pl.BlockSpec(memory_space=pltpu.VMEM)
+SMEM_SPEC = pl.BlockSpec(memory_space=pltpu.SMEM)
+ANY_SPEC = pl.BlockSpec(memory_space=pl.ANY)
+LINE = pltpu.VMEM((4, round_up(max(D, DI), 8), LANES), jnp.float32)
+
+
+def shape_of(shape, dtype=low):
+    return jax.ShapeDtypeStruct(shape, dtype)
+
+
+def shards_of(n_head, shard_rows, first, last):
+    starts = borders(n_head)
+    begin = starts[first] // shard_rows
+    return begin, -(-starts[last] // shard_rows) - begin
+
+
+def encode(bounds, weights, common, inputs, rows, n_head, shard_rows):
+    width = HEADS // n_head * HD
+    begin, shards = shards_of(n_head, shard_rows, 0, 4)
+    common_rows = common.shape[0] - DQ * D // LANES // TILE * TILE
+    keys = inputs.shape[0]
+    return pl.pallas_call(
+        functools.partial(encode_kernel, n_head, shard_rows, rows),
+        out_shape=[
+            shape_of((D, D)),
+            shape_of((DI, 2 * D)),
+            shape_of((D, D)),
+            shape_of((D, 3 * D)),
+            shape_of((4, D), jnp.float32),
+            shape_of((rows, D), jnp.float32),
+            shape_of((rows, D)),
+            shape_of(inputs.shape),
+            shape_of((rows, D)),
+            shape_of((keys, 2 * D)),
+            shape_of((rows, D)),
+            shape_of((rows, D), jnp.float32),
+            shape_of((rows, D)),
+            shape_of((n_head, rows, width)),
+            shape_of((n_head, rows, 2 * width)),
+        ],
+        in_specs=[SMEM_SPEC, ANY_SPEC, ANY_SPEC, VMEM_SPEC],
+        out_specs=[VMEM_SPEC] * 15,
+        scratch_shapes=[
+            pltpu.VMEM((shards,) + weights.shape[1:], low),
+            pltpu.VMEM((common_rows, LANES), low),
+            pltpu.VMEM((shards * shard_rows, LANES), jnp.float32),
+            pltpu.VMEM((common_rows, LANES), jnp.float32),
+            LINE,
+            pltpu.VMEM((LAT, D), low),
+            pltpu.SemaphoreType.DMA((2,)),
+        ],
+        compiler_params=pltpu.CompilerParams(vmem_limit_bytes=56 * MIB),
+        name="encode",
+    )(bounds, weights, common, inputs)
+
+
+def gelu_and_slope(x):
+    rate = (2.0 / jnp.pi) ** 0.5
+    cubic = 0.044715
+    t = jnp.tanh(rate * (x + cubic * x * x * x))
+    slope = 0.5 * (1.0 + t) + 0.5 * x * (1.0 - t * t) * rate * (1.0 + 3.0 * cubic * x * x)
+    return 0.5 * x * (1.0 + t), slope
+
+
+def middle_kernel(
+    n_head,
+    shard_rows,
+    first_shard,
+    rows,
+    counts,
+    weights,
+    common,
+    z_one,
+    o_self,
+    out_queries,
+    marks,
+    gains,
+    dout,
+    d_two_out,
+    tile,
+    query_grad,
+    gain_grads,
+    grads,
+    held,
+    held_common,
+    stage,
+    stage_common,
+    line,
+    self_output,
+    hidden_in,
+    hidden_out,
+    class_table,
+    query_table,
+    slope,
+    activ,
+    sems,
+):
+    heads = HEADS // n_head
+    width, hidden, classes = heads * HD, FF // n_head, C // n_head
+    shards = held.shape[0]
+    first_row = first_shard * shard_rows
+    starts = borders(n_head)
+    copies = [
+        pltpu.make_async_copy(common.at[pl.ds(0, held_common.shape[0])], held_common, sems.at[0]),
+        pltpu.make_async_copy(weights.at[pl.ds(first_shard, shards)], held, sems.at[1]),
+    ]
+    for copy in copies:
+        copy.start()
+    copies[0].wait()
+    stage_common[...] = held_common[...].astype(jnp.float32)
+    for j, value in matrix_of(stage_common, 0, DQ, D, line):
+        query_table[:, j : j + LANES] = value.astype(low)
+    copies[1].wait()
+    for g in range(n_head):
+        load_stage(stage, held, first_shard, shard_rows, g)
+        load_matrices(
+            stage, first_row, n_head, g, (4, 5, 6, 7), (self_output, hidden_in, hidden_out, class_table), line
+        )
+    gain_two, gain_three = gains[2:3, :], gains[3:4, :]
+    o_low = jnp.concatenate([o_self[g] for g in range(n_head)], 1)
+    z_two = z_one[...] + product(o_low, self_output[...])
+    h_two = layer_norm(z_two, gain_two).astype(low)
+    value, bend = gelu_and_slope(product(h_two, hidden_in[...]))
+    activ[...] = value.astype(low)
+    slope[...] = bend
+    z_three = z_two + product(activ[...], hidden_out[...])
+    queries = out_queries[...]
+    decoded = (layer_norm(z_three, gain_three) + product(queries, query_table[...])).astype(low)
+    logits = product(decoded, class_table[...])
+    at = pl.multiple_of(lax.axis_index("head") * rows, rows)
+    mark = marks[:, pl.ds(at, rows)].T
+    label, kind, counted = (mark[:, i : i + 1] for i in range(3))
+    lane = lax.broadcasted_iota(jnp.int32, (rows, C), 1).astype(jnp.float32)
+    is_target = jnp.where(lane == label, 1.0, 0.0)
+    row_top = jnp.max(logits, 1, keepdims=True)
+    row_lse = row_top + jnp.log(jnp.sum(jnp.exp(logits - row_top), 1, keepdims=True))
+    loss = row_lse - jnp.sum(is_target * logits, 1, keepdims=True)
+    weight = jnp.zeros((rows, 1), jnp.float32)
+    place = lax.broadcasted_iota(jnp.int32, (1, LANES), 1)
+    losses = jnp.zeros((1, LANES), jnp.float32)
+    for m in range(MODES):
+        member = jnp.where((kind == m) & (counted == 1.0), 1.0, 0.0)
+        weight = weight + member / jnp.maximum(counts[m], 1.0)
+        losses = losses + jnp.where(place == m, jnp.sum(loss * member, 0, keepdims=True), 0.0)
+    tile[...] = jnp.broadcast_to(losses, tile.shape)
+    dlogits = (weight * (jnp.exp(logits - row_lse) - is_target)).astype(low)
+    d_decoded = against(dlogits, class_table[...])
+    table_grad = contract_first(queries, d_decoded.astype(low))
+    matrix_into(stage_common, 0, table_grad, line)
+    query_grad[...] = stage_common[: query_grad.shape[0], :].astype(low)
+    d_three, gain_three_grad = norm_pullback(z_three, gain_three, d_decoded)
+    d_branch = d_three.astype(low)
+    d_pre = (slope[...] * against(d_branch, hidden_out[...])).astype(low)
+    d_middle, gain_two_grad = norm_pullback(z_two, gain_two, against(d_pre, hidden_in[...]))
+    d_two = d_three + d_middle
+    d_two_out[...] = d_two
+    gain_grads[...] = jnp.concatenate([gain_two_grad, gain_three_grad], 0)
+    d_two_low = d_two.astype(low)
+    d_o = against(d_two_low, self_output[...]).astype(low)
+    for g in range(n_head):
+        dout[g] = d_o[:, g * width : (g + 1) * width]
+    for g in range(n_head):
+        results = (
+            contract_first(o_self[g], d_two_low),
+            contract_first(h_two, d_pre[:, g * hidden : (g + 1) * hidden]),
+            contract_first(activ[:, g * hidden : (g + 1) * hidden], d_branch),
+            contract_first(decoded, dlogits[:, g * classes : (g + 1) * classes]),
+        )
+        for m, result in zip((4, 5, 6, 7), results):
+            matrix_into(stage, starts[m] - first_row, result, line)
+        for b in range(shards):
+            held[b, g, :shard_rows, :] = stage[pl.ds(b * shard_rows, shard_rows), :].astype(low)
+    back = pltpu.make_async_copy(held, grads.at[pl.ds(first_shard, shards)], sems.at[2])
+    back.start()
+    back.wait()
+
+
+def middle(counts, weights, common, z_one, o_self, out_queries, marks, gains, n_head, shard_rows):
+    rows = z_one.shape[0]
+    begin, shards = shards_of(n_head, shard_rows, 4, 8)
+    query_rows = DQ * D // LANES
+    common_rows = round_up(query_rows, TILE)
+    return pl.pallas_call(
+        functools.partial(middle_kernel, n_head, shard_rows, begin, rows),
+        grid=(1,),
+        out_shape=[
+            shape_of(o_self.shape),
+            shape_of((rows, D), jnp.float32),
+            shape_of((8, LANES), jnp.float32),
+            shape_of((query_rows, LANES)),
+            shape_of((2, D), jnp.float32),
+            shape_of(weights.shape),
+        ],
+        in_specs=[
+            SMEM_SPEC,
+            ANY_SPEC,
+            ANY_SPEC,
+            VMEM_SPEC,
+            VMEM_SPEC,
+            pl.BlockSpec((rows, DQ), lambda i: (lax.axis_index("head"), 0)),
+            VMEM_SPEC,
+            VMEM_SPEC,
+        ],
+        out_specs=[VMEM_SPEC] * 5 + [ANY_SPEC],
+        scratch_shapes=[
+            pltpu.VMEM((shards,) + weights.shape[1:], low),
+            pltpu.VMEM((common_rows, LANES), low),
+            pltpu.VMEM((shards * shard_rows, LANES), jnp.float32),
+            pltpu.VMEM((common_rows, LANES), jnp.float32),
+            LINE,
+            pltpu.VMEM((D, D), low),
+            pltpu.VMEM((D, FF), low),
+            pltpu.VMEM((FF, D), low),
+            pltpu.VMEM((D, C), low),
+            pltpu.VMEM((DQ, D), low),
+            pltpu.VMEM((rows, FF), jnp.float32),
+            pltpu.VMEM((rows, FF), low),
+            pltpu.SemaphoreType.DMA((3,)),
+        ],
+        compiler_params=pltpu.CompilerParams(vmem_limit_bytes=56 * MIB),
+        name="middle",
+    )(counts, weights, common, z_one, o_self, out_queries, marks, gains)
+
+
+def ending_kernel(
+    n_head,
+    shard_rows,
+    rows,
+    bounds,
+    grads_in,
+    d_projected,
+    d_two,
+    gains,
+    gain_grads,
+    enc_query,
+    enc_keyval,
+    enc_output,
+    self_project,
+    z_zero,
+    h_zero,
+    x_norm,
+    q_enc,
+    kv_enc,
+    o_enc,
+    z_one,
+    h_one,
+    grads,
+    tail_grad,
+    held,
+    stage,
+    stage_common,
+    line,
+    d_q,
+    d_kv,
+    sems,
+):
+    heads = HEADS // n_head
+    width = heads * HD
+    shards = held.shape[0]
+    starts = borders(n_head)
+    shared = pltpu.make_async_copy(grads_in.at[pl.ds(shards - 1, 1)], held.at[pl.ds(shards - 1, 1)], sems.at[0])
+    shared.start()
+    whole = jnp.concatenate([d_projected[g] for g in range(n_head)], 1)
+    d_middle, gain_one_grad = norm_pullback(
+        z_one[...], gains[1:2, :], against(whole, self_project[...])
+    )
+    d_one = d_two[...] + d_middle
+    d_one_low = d_one.astype(low)
+    d_o = against(d_one_low, enc_output[...]).astype(low)
+    for g in range(n_head):
+        keys = kv_enc[:, 2 * g * width : (2 * g + 1) * width]
+        values = kv_enc[:, (2 * g + 1) * width : (2 * g + 2) * width]
+        d_key = jnp.zeros(keys.shape, jnp.float32)
+        d_value = jnp.zeros(keys.shape, jnp.float32)
+        d_query = jnp.zeros((rows, width), jnp.float32)
+        for (here, q_head), (unused, do_head) in zip(
+            head_lanes(g, heads, q_enc[...]), head_lanes(g, heads, d_o)
+        ):
+            scores = enc_scores(keys, q_head)
+            probs = jnp.exp(scores - jnp.max(scores, 0, keepdims=True))
+            probs = probs / jnp.sum(probs, 0, keepdims=True)
+            d_probs = against(values, do_head)
+            delta = jnp.sum(probs * d_probs, 0, keepdims=True)
+            d_scores = (probs * (d_probs - delta)).astype(low)
+            d_value = d_value + product(probs.astype(low), do_head)
+            d_key = d_key + product(d_scores, q_head)
+            d_query = jnp.where(here, contract_first(d_scores, keys), d_query)
+        d_q[:, g * width : (g + 1) * width] = (d_query * HD ** (-0.5)).astype(low)
+        d_kv[:, 2 * g * width : (2 * g + 1) * width] = (d_key * HD ** (-0.5)).astype(low)
+        d_kv[:, (2 * g + 1) * width : (2 * g + 2) * width] = d_value.astype(low)
+    d_middle, gain_zero_grad = norm_pullback(
+        z_zero[...], gains[0:1, :], against(d_q[...], enc_query[...])
+    )
+    d_zero = d_one + d_middle
+    d_zero_top = d_zero.astype(low)
+    d_zero_rest = (d_zero - d_zero_top.astype(jnp.float32)).astype(low)
+    picked = picked_rows(bounds, rows, n_head)
+    latent_grad = contract_first(picked, d_zero_top) + contract_first(picked, d_zero_rest)
+    matrix_into(stage_common, 0, latent_grad, line)
+    all_gains = jnp.concatenate([gain_zero_grad, gain_one_grad, gain_grads[...]], 0)
+    matrix_into(stage_common, LAT * D // LANES, all_gains, line)
+    tail_grad[...] = stage_common[...].astype(low)
+    shared.wait()
+    kept = shards * shard_rows - starts[4]
+    for g in range(n_head):
+        results = (
+            contract_first(h_zero[...], d_q[:, g * width : (g + 1) * width]),
+            contract_first(x_norm[...], d_kv[:, 2 * g * width : (2 * g + 2) * width]),
+            contract_first(o_enc[:, g * width : (g + 1) * width], d_one_low),
+            contract_first(h_one[...], d_projected[g]),
+        )
+        if kept:
+            stage[pl.ds((shards - 1) * shard_rows, shard_rows), :] = held[
+                shards - 1, g, :shard_rows, :
+            ].astype(jnp.float32)
+        for m, result in zip((0, 1, 2, 3), results):
+            matrix_into(stage, starts[m], result, line)
+        for b in range(shards):
+            held[b, g, :shard_rows, :] = stage[pl.ds(b * shard_rows, shard_rows), :].astype(low)
+    back = pltpu.make_async_copy(held, grads.at[pl.ds(0, shards)], sems.at[1])
+    back.start()
+    back.wait()
+
+
+def ending(bounds, grads, d_projected, d_two, gains, gain_grads, kept, n_head, shard_rows):
+    rows = d_two.shape[0]
+    begin, shards = shards_of(n_head, shard_rows, 0, 4)
+    keys = kept[6].shape[0]
+    tail_rows = (LAT + 4) * D // LANES
+    return pl.pallas_call(
+        functools.partial(ending_kernel, n_head, shard_rows, rows),
+        out_shape=[shape_of(grads.shape), shape_of((tail_rows, LANES))],
+        in_specs=[SMEM_SPEC, ANY_SPEC] + [VMEM_SPEC] * 16,
+        out_specs=[ANY_SPEC, VMEM_SPEC],
+        input_output_aliases={1: 0},
+        scratch_shapes=[
+            pltpu.VMEM((shards,) + grads.shape[1:], low),
+            pltpu.VMEM((shards * shard_rows, LANES), jnp.float32),
+            pltpu.VMEM((tail_rows, LANES), jnp.float32),
+            LINE,
+            pltpu.VMEM((rows, D), low),
+            pltpu.VMEM((keys, 2 * D), low),
+            pltpu.SemaphoreType.DMA((2,)),
+        ],
+        compiler_params=pltpu.CompilerParams(vmem_limit_bytes=56 * MIB),
+        name="ending",
+    )(bounds, grads, d_projected, d_two, gains, gain_grads, *kept)
 
 
 def adam_step(weight, first, second, grad):
@@ -775,189 +1383,78 @@
 ):
     n_head, n_blk = lax.axis_size("head"), lax.axis_size("blk")
     dims = grid_of(n_blk, n_head)
-    head_rank, blk_rank = lax.axis_index("head"), lax.axis_index("blk")
+    head_rank = lax.axis_index("head")
     blk_rows = labels.shape[0]
     rows = blk_rows // n_head
     heads_here = HEADS // n_head
     width = heads_here * HD
     n_h, n_c = head_params.shape[0], common_params.shape[0]
-    head_rows = round_up(-(-n_h // LANES), TILE)
+    shard_rows = n_h // LANES
+    head_rows = round_up(shard_rows + 1, TILE)
     piece_rows = round_up(-(-(-(-n_c // LANES)) // n_head), TILE)
 
-    def mine(x):
-        return lax.dynamic_slice_in_dim(x, head_rank * rows, rows, 0)
-
-    head_low = jnp.pad(head_params.astype(low), (0, head_rows * LANES - n_h)).reshape(head_rows, LANES)
+    marks = jnp.stack([labels, modality, labeled] + [jnp.zeros_like(labels)] * 5).astype(jnp.float32)
+    mine = lax.dynamic_slice_in_dim(marks, head_rank * rows, rows, 1)
+    member = (mine[1][None] == jnp.arange(MODES, dtype=jnp.float32)[:, None]) & (mine[2][None] == 1.0)
+    counted = jnp.pad(jnp.sum(member.astype(jnp.float32), 1), (0, LANES - MODES)).astype(low)
+    head_low = jnp.concatenate(
+        [
+            head_params.astype(low).reshape(shard_rows, LANES),
+            jnp.broadcast_to(counted[None], (head_rows - shard_rows, LANES)),
+        ]
+    )
     common_low = jnp.pad(common_params.astype(low), (0, n_head * piece_rows * LANES - n_c))
     common_low = lax.dynamic_slice_in_dim(
         common_low.reshape(n_head * piece_rows, LANES), head_rank * piece_rows, piece_rows, 0
     )
-    everything = gather_all(dims, jnp.concatenate([head_low, common_low], 0), 0)
-    head_flat = [
-        everything[:, g, :head_rows].reshape(n_blk, head_rows * LANES)[:, :n_h].reshape(-1)
-        for g in range(n_head)
-    ]
-    common_flat = everything[:, :, head_rows:].reshape(n_blk, n_head * piece_rows * LANES)[:, :n_c]
-    common_flat = common_flat.reshape(-1)
-    shapes = part_shapes(n_head)
-    parts = []
-    border = 0
-    for shape in shapes:
-        amount = shape[0] * shape[1]
-        parts.append([flat[border : border + amount].reshape(shape) for flat in head_flat])
-        border += amount
-    enc_query = jnp.concatenate(parts[0], 1)
-    enc_key = jnp.concatenate([w[:, :width] for w in parts[1]], 1)
-    enc_value = jnp.concatenate([w[:, width:] for w in parts[1]], 1)
-    enc_output = jnp.concatenate(parts[2], 0)
-    self_project = jnp.concatenate(parts[3], 1)
-    self_output = jnp.concatenate(parts[4], 0)
-    hidden_in = jnp.concatenate(parts[5], 1)
-    hidden_out = jnp.concatenate(parts[6], 0)
-    class_table = jnp.concatenate(parts[7], 1)
-    query_table = common_flat[: DQ * D].reshape(DQ, D)
-    latent_table = common_flat[DQ * D : (DQ + LAT) * D].reshape(LAT, D)
-    norm_gains = common_flat[(DQ + LAT) * D :].reshape(4, D).astype(jnp.float32)
+    weights, common = gather_all(dims, (head_low, common_low), 0)
+    label_counts = jnp.sum(weights[:, :, shard_rows, :MODES].astype(jnp.float32), (0, 1))
+    if n_c % LANES == 0:
+        common = common.reshape(n_blk, n_head * piece_rows, LANES)[:, : n_c // LANES]
+    else:
+        common = common.reshape(n_blk, n_head * piece_rows * LANES)[:, :n_c]
+    common = common.reshape(-1, LANES)
+    common = jnp.pad(common, ((0, -common.shape[0] % TILE), (0, 0)))
 
     finish = jnp.cumsum(clip_lengths)
     bounds = jnp.stack([finish - clip_lengths, finish])
-    places = blk_rank * blk_rows + head_rank * rows + jnp.arange(rows, dtype=jnp.int32)
-    inside = (places[:, None] >= bounds[0][None]) & (places[:, None] < bounds[1][None])
-    offset = places - jnp.sum(jnp.where(inside, bounds[0][None], 0), 1)
-    latent_rows = offset % LAT
-    picked = (latent_rows[:, None] == jnp.arange(LAT, dtype=jnp.int32)[None]).astype(low)
-    labels, modality, labeled = mine(labels), mine(modality), mine(labeled)
-    out_queries = mine(out_queries)
-
-    def split(x):
-        return x.reshape(x.shape[0], HEADS, HD)
-
-    z_zero = product(picked, latent_table)
-    h_zero = layer_norm(z_zero, norm_gains[0]).astype(low)
-    x_norm = layer_norm(inputs.astype(jnp.float32), 1.0).astype(low)
-    q_enc = split(product(h_zero, enc_query).astype(low))
-    k_enc = split(product(x_norm, enc_key).astype(low))
-    v_enc = split(product(x_norm, enc_value).astype(low))
-
-    def scores_of(q, k):
-        return jnp.einsum("qhd,khd->hqk", q, k, preferred_element_type=jnp.float32) * HD ** (-0.5)
-
-    p_enc = jax.nn.softmax(scores_of(q_enc, k_enc), axis=-1)
-    o_enc = jnp.einsum("hqk,khd->qhd", p_enc.astype(low), v_enc, preferred_element_type=jnp.float32)
-    o_enc_low = o_enc.reshape(rows, HEADS * HD).astype(low)
-    z_one = z_zero + product(o_enc_low, enc_output)
-    h_one = layer_norm(z_one, norm_gains[1]).astype(low)
-    projected = product(h_one, self_project).astype(low).reshape(rows, n_head, 3 * width)
-    projected = projected.transpose(1, 0, 2)
-    q_self, kv_self = spread_rows(dims, projected[:, :, :width], projected[:, :, width:], 1)
+    encoded = encode(bounds, weights, common, inputs, rows, n_head, shard_rows)
+    gains, z_one = encoded[4], encoded[11]
+    q_self, kv_self = spread_rows(dims, encoded[13], encoded[14], 1)
     q_self = q_self.reshape(blk_rows, width)
     kv_self = kv_self.reshape(n_blk * blk_rows, 2 * width)
     out_self, lse_self, out_self_t = attend(bounds, q_self, kv_self, heads_here)
-    o_self_low = swap_heads(dims, out_self.reshape(n_head, rows, width), 2)
-    o_self_low = o_self_low.transpose(1, 0, 2).reshape(rows, HEADS * HD)
-    z_two = z_one + product(o_self_low, self_output)
-    h_two = layer_norm(z_two, norm_gains[2]).astype(low)
-    pre_act = product(h_two, hidden_in)
-    activ = jax.nn.gelu(pre_act).astype(low)
-    z_three = z_two + product(activ, hidden_out)
-    decoded_low = (layer_norm(z_three, norm_gains[3]) + product(out_queries, query_table)).astype(low)
-    logits = product(decoded_low, class_table)
-    is_target = (labels[:, None] == jnp.arange(C, dtype=jnp.int32)[None, :]).astype(jnp.float32)
-    row_top = jnp.max(logits, -1, keepdims=True)
-    row_lse = row_top + jnp.log(jnp.sum(jnp.exp(logits - row_top), -1, keepdims=True))
-    target = jnp.sum(is_target * logits, -1, keepdims=True)
-    member = (
-        (modality[:, None] == jnp.arange(MODES, dtype=jnp.int32)[None, :]) & (labeled[:, None] == 1)
-    ).astype(jnp.float32)
-    label_counts = lax.psum(jnp.sum(member, 0), ("blk", "head"))
-    loss_sums = lax.psum(jnp.sum((row_lse - target) * member, 0), ("blk", "head"))
-
-    row_weight = jnp.sum(member / jnp.maximum(label_counts, 1.0)[None, :], 1, keepdims=True)
-    dlogits = (row_weight * (jnp.exp(logits - row_lse) - is_target)).astype(low)
-    class_grad = inner(decoded_low, dlogits)
-    d_decoded = against(dlogits, class_table)
-    query_grad = inner(out_queries, d_decoded.astype(low))
-    d_three, gain_three = norm_pullback(z_three, norm_gains[3], d_decoded)
-    d_branch = d_three.astype(low)
-    out_grad = inner(activ, d_branch)
-    unused, gelu_pull = jax.vjp(jax.nn.gelu, pre_act)
-    d_pre = gelu_pull(against(d_branch, hidden_out))[0].astype(low)
-    in_grad = inner(h_two, d_pre)
-    d_middle, gain_two = norm_pullback(z_two, norm_gains[2], against(d_pre, hidden_in))
-    d_two = d_three + d_middle
-    d_branch = d_two.astype(low)
-    self_out_grad = inner(o_self_low, d_branch)
-    dout_self = against(d_branch, self_output).astype(low)
-    dout_self = swap_heads(
-        dims, dout_self.reshape(rows, n_head, width).transpose(1, 0, 2), 3
-    ).reshape(blk_rows, width)
-    d_q, d_kv = attend_back(bounds, q_self, kv_self, dout_self, out_self_t, lse_self, heads_here)
+    o_self = swap_heads(dims, out_self.reshape(n_head, rows, width), 2)
+    dout, d_two, tile, query_grad, gain_grads, grads = middle(
+        label_counts, weights, common, z_one, o_self, out_queries, marks, gains, n_head, shard_rows
+    )
+    dout = swap_heads(dims, dout, 3).reshape(blk_rows, width)
+    d_q, d_kv = attend_back(bounds, q_self, kv_self, dout, out_self_t, lse_self, heads_here)
     d_kv = collect_rows(dims, d_kv.reshape(n_blk, blk_rows, 2 * width), 4)
     d_projected = swap_heads(
         dims, jnp.concatenate([d_q, d_kv], 1).reshape(n_head, rows, 3 * width), 5
     )
-    d_projected = d_projected.transpose(1, 0, 2).reshape(rows, n_head * 3 * width)
-    project_grad = inner(h_one, d_projected)
-    d_middle, gain_one = norm_pullback(z_one, norm_gains[1], against(d_projected, self_project))
-    d_one = d_two + d_middle
-    d_branch = d_one.astype(low)
-    enc_out_grad = inner(o_enc_low, d_branch)
-    dout_enc = split(against(d_branch, enc_output).astype(low))
-    dp_enc = jnp.einsum("qhd,khd->hqk", dout_enc, v_enc, preferred_element_type=jnp.float32)
-    delta_enc = jnp.einsum("qhd,qhd->hq", dout_enc.astype(jnp.float32), o_enc)
-    ds_enc = (p_enc * (dp_enc - delta_enc[..., None])).astype(low)
-    d_q_enc = jnp.einsum("hqk,khd->qhd", ds_enc, k_enc, preferred_element_type=jnp.float32) * HD ** (-0.5)
-    d_k_enc = jnp.einsum("hqk,qhd->khd", ds_enc, q_enc, preferred_element_type=jnp.float32) * HD ** (-0.5)
-    d_v_enc = jnp.einsum(
-        "hqk,qhd->khd", p_enc.astype(low), dout_enc, preferred_element_type=jnp.float32
-    )
-    d_q_enc, d_k_enc, d_v_enc = (x.reshape(-1, HEADS * HD).astype(low) for x in (d_q_enc, d_k_enc, d_v_enc))
-    enc_query_grad = inner(h_zero, d_q_enc)
-    enc_key_grad = inner(x_norm, d_k_enc)
-    enc_value_grad = inner(x_norm, d_v_enc)
-    d_middle, gain_zero = norm_pullback(z_zero, norm_gains[0], against(d_q_enc, enc_query))
-    d_zero = d_one + d_middle
-    d_zero_top = d_zero.astype(low)
-    d_zero_rest = (d_zero - d_zero_top.astype(jnp.float32)).astype(low)
-    latent_grad = inner(picked, d_zero_top) + inner(picked, d_zero_rest)
-
-    def columns(whole, g):
-        size = whole.shape[1] // n_head
-        return whole[:, g * size : (g + 1) * size]
-
-    def of_rows(whole, g):
-        size = whole.shape[0] // n_head
-        return whole[g * size : (g + 1) * size]
-
-    flat = []
-    for g in range(n_head):
-        group = [
-            columns(enc_query_grad, g),
-            jnp.concatenate([columns(enc_key_grad, g), columns(enc_value_grad, g)], 1),
-            of_rows(enc_out_grad, g),
-            columns(project_grad, g),
-            of_rows(self_out_grad, g),
-            columns(in_grad, g),
-            of_rows(out_grad, g),
-            columns(class_grad, g),
-        ]
-        flat.append(jnp.concatenate([w.astype(low).reshape(-1) for w in group]).reshape(n_blk, n_h))
-    flat = jnp.pad(jnp.stack(flat, 1), ((0, 0), (0, 0), (0, head_rows * LANES - n_h)))
-    gains = jnp.stack([gain_zero, gain_one, gain_two, gain_three])
-    common = jnp.concatenate([w.astype(low).reshape(-1) for w in (query_grad, latent_grad, gains)])
-    common = jnp.pad(common.reshape(n_blk, n_c), ((0, 0), (0, n_head * piece_rows * LANES - n_c)))
-    blocks = jnp.concatenate(
-        [
-            flat.reshape(n_blk, n_head, head_rows, LANES),
-            common.reshape(n_blk, n_head, piece_rows, LANES),
-        ],
-        2,
-    )
-    share = reduce_all(dims, blocks, 6)
-    clip_norm = jnp.sqrt(lax.psum(jnp.sum(share * share), ("blk", "head")))
+    kept = encoded[:4] + encoded[5:13]
+    grads, tail_grad = ending(
+        bounds, grads, d_projected, d_two, gains, gain_grads, kept, n_head, shard_rows
+    )
+    common_grad = jnp.concatenate([query_grad, tail_grad])
+    space = n_head * piece_rows * LANES
+    if n_c % LANES == 0:
+        common_grad = jnp.pad(
+            common_grad.reshape(n_blk, n_c // LANES, LANES),
+            ((0, 0), (0, (space - n_c) // LANES), (0, 0)),
+        )
+    else:
+        common_grad = jnp.pad(common_grad.reshape(n_blk, n_c), ((0, 0), (0, space - n_c)))
+    common_grad = common_grad.reshape(n_blk, n_head, piece_rows, LANES)
+    head_share, unused, totals, common_share = reduce_all(
+        dims, (grads, common_grad), (shard_rows, piece_rows), tile, 6
+    )
+    clip_norm = jnp.sqrt(totals[0, MODES])
+    loss_sums = totals[0, :MODES]
     factor = jnp.minimum(1.0, clip_limit / clip_norm)
-    head_share = share[:head_rows].reshape(-1)[:n_h]
-    common_share = lax.all_gather(share[head_rows:].astype(low), "head", axis=0, tiled=True)
+    head_share = head_share[:shard_rows].reshape(-1)
     common_share = common_share.reshape(-1)[:n_c].astype(jnp.float32)
     head_out = adam_step(head_params, head_first, head_second, head_share * factor)
     common_out = adam_step(common_params, common_first, common_second, common_share * factor)

time: 892 us -> 531 us (0.60)
  local copies, waits for them, and re-layouts: 275 us -> 19.9 us
  blocking collectives: 94.8 us -> 0 us
  Pallas kernels: 411 us -> 492 us
  matrix products: 53.2 us -> 0 us
  other arithmetic: 42.5 us -> 13.3 us
    slice x56 -> x3, local copies, waits for them, and re-layouts: 130 us -> 3.11 us  [the longest x1 1.64 us: per_device(): common = common.reshape(n_blk, n_head * piece_rows, LANES)[:, :n_c // LANES]]
    psum x2 -> x0, blocking collectives: 88.2 us -> none  [the longest x1 46.2 us: per_device(): clip_norm = jnp.sqrt(lax.psum(jnp.sum(share * share), ('blk', 'head')))]
    pallas_call x2 -> x5, Pallas kernels: 135 us -> 205 us  [the longest x1 94.4 us: reduce_all(): pl.pallas_call(functools.partial(reduce_kernel, dims, parts, row_chunk, v...]
    unnamed x348 -> x26, local copies, waits for them, and re-layouts: 69.2 us -> 5.99 us
    dot_general x35 -> x0, matrix products: 48.4 us -> none  [the longest x12 13.5 us: inner(): lax.dot_general(a, b, (((0,), (0,)), ((), ())), preferred_element_type=jn...]
    another operation x6 -> x3, local copies, waits for them, and re-layouts: 32.1 us -> 0.76 us  [per_device(): jnp.stack([labels, modality, labeled] + [jnp.zeros_like(labels)] * 5)]
    reshape x25 -> x2, local copies, waits for them, and re-layouts: 32.7 us -> 3.86 us  [the longest x1 2.06 us: per_device(): common_grad.reshape(n_blk, n_c // LANES, LANES)]
    pallas_call x1, Pallas kernels: 72.4 us -> 82.5 us  [collect_rows(): pl.pallas_call(functools.partial(collect_kernel, dims), out_shape=jax.Sha...]
where the time goes in v2:
time: 531 us; the launch traced here: 528 us
  Pallas kernels  492 us (93%)
  local copies, waits for them, and re-layouts  19.9 us (4%)
  other arithmetic  13.3 us (3%)
    pallas_call x1, Pallas kernels, reduce_all(): pl.pallas_call(functools.partial(reduce_kernel, dims, parts, row_chunk, v...  94.4 us
    pallas_call x1, Pallas kernels, collect_rows(): pl.pallas_call(functools.partial(collect_kernel, dims), out_shape=jax.Sha...  82.5 us
    pallas_call x1, Pallas kernels, spread_rows(): pl.pallas_call(functools.partial(spread_kernel, dims), out_shape=(jax.Sha...  70.9 us
    pallas_call x1, Pallas kernels, gather_all(): pl.pallas_call(functools.partial(gather_kernel, dims, parts, len(shards))...  64.9 us
    pallas_call x1, Pallas kernels, attend_back(): pl.pallas_call(functools.partial(attend_back_kernel, heads, key_step), ou...  56 us
    pallas_call x1, Pallas kernels, attend(): pl.pallas_call(functools.partial(attend_kernel, heads, key_step, query_st...  54.8 us
    pallas_call x3, Pallas kernels, swap_heads(): pl.pallas_call(functools.partial(swap_kernel, dims), out_shape=jax.ShapeD...  22.9 us
    pallas_call x1, Pallas kernels, middle(): pl.pallas_call(functools.partial(middle_kernel, n_head, shard_rows, begin...  17.9 us

profile of v2, /device:TPU:0, one launch (start us, length us, event | category | flops | bytes accessed | tf_op | source)
XLA Modules:
  0.0 528.3 jit_solution(5496953145756708193)
XLA Ops:
  0.6 0.0 copy-start.1
  0.7 0.0 copy-start.5
  0.7 0.9 reduce-window.4
  1.6 0.7 fusion.4
  2.3 0.6 pad_add_fusion.bounds
  2.9 0.8 stack.31
  3.6 0.1 compare_reduce_fusion
  3.7 0.1 dynamic-slice
  3.8 0.1 convert_reduce_fusion.1
  4.0 1.0 convert_element_type.37
  5.0 0.0 copy-start.2
  5.1 0.6 constant_dynamic-slice_fusion.refs_1_
  5.7 0.7 pad_maximum_fusion.2.refs_0_
  6.5 0.0 copy-done.5
  6.5 1.2 copy.28.inputs
  7.6 0.0 copy-done.11
  7.6 2.6 copy.29.out_queries
  10.2 64.9 %gather_weights.1 = (bf16[8,4,1168,128]{3,2,1,0:T(8,128)(2,1)}, bf16[8,4,240,128]{3,2,1,0:T(8,128)(2,1)}) custom-call(bf16[1168,128]{1,0:T(8,128)(2,1)} %pad_maximum_fusion.2.refs_0_, bf16[240,128]{1,0:T(8,128)(2,1)} %constant_dynamic-slice_fusion.refs_1_), custom_call_target="tpu_custom_call" | custom-call | tf_op jit(solution)/shard_map/gather_weights/pallas_call | solution.py:192
  75.1 1.6 slice.32
  76.7 1.8 reshape.79
  78.5 1.4 convert_reduce_fusion.counts
  79.9 2.9 pad.19.common
  82.8 11.2 %encode.1 = (bf16[512,512]{1,0:T(8,128)(2,1)}, bf16[704,1024]{1,0:T(8,128)(2,1)}, bf16[512,512]{1,0:T(8,128)(2,1)}, bf16[512,1536]{1,0:T(8,128)(2,1)}, f32[4,512...) custom-call(s32[2,6]{1,0:T(2,128)} %pad_add_fusion.bounds, ...), custom_call_target="tpu_custom_call" | custom-call | tf_op jit(solution)/shard_map/encode/pallas_call | solution.py:1031
  94.1 70.9 %spread_rows.1 = (bf16[4,256,128]{2,1,0:T(8,128)(2,1)}, bf16[8,4,256,256]{3,2,1,0:T(8,128)(2,1)}) custom-call(bf16[4,256,128]{2,1,0:T(8,128)(2,1)} %get-tuple-element.49.q_in, bf16[4,256,256]{2,1,0:T(8,128)(2,1)} %get-tuple-element.50.kv_in), custom_call_target="tpu_custom_call" | custom-call | tf_op jit(solution)/shard_map/spread_rows/pallas_call | solution.py:441
  165.0 54.8 %attend.1 = (bf16[1024,128]{1,0:T(8,128)(2,1)}, f32[2,1024]{1,0:T(2,128)}, f32[128,1024]{1,0:T(8,128)}) custom-call(s32[2,6]{1,0:T(2,128)} %pad_add_fusion.bounds, bf16[1024,128]{1,0:T(8,128)(2,1)} %bitcast.41, bf16[8192,256]{1,0:T(8,128)(2,1)} %bitcast.36), custom_call_target="tpu_custom_call" | custom-call | tf_op jit(solution)/shard_map/attend/pallas_call | solution.py:684
  219.8 5.7 %swap_heads.3.o_self = bf16[4,256,128]{2,1,0:T(8,128)(2,1)} custom-call(bf16[4,256,128]{2,1,0:T(8,128)(2,1)} %bitcast.44), custom_call_target="tpu_custom_call" | custom-call | tf_op jit(solution)/shard_map/swap_heads/pallas_call | solution.py:484
  225.5 17.9 %middle.1 = (bf16[4,256,128]{2,1,0:T(8,128)(2,1)}, f32[256,512]{1,0:T(8,128)}, f32[8,128]{1,0:T(8,128)}, bf16[4104,128]{1,0:T(8,128)(2,1)}, f32[2,512]{1,0:T(2,128)}, /*index=5*/bf16[8,4,1168,128]{3,2,1,0:T(8,128)(2,1)}) custom-call(f32[3]{0:T(128)} %convert_reduce_fusion.counts, bf16[8,4,1168,128]{3,2,1,0:T(8,128)(2,1)} %get-tuple-element.46.weights, ...), custom_call_target="tpu_custom_call" | custom-call | tf_op jit(solution)/shard_map/middle/pallas_call | solution.py:1192
  243.5 5.8 %swap_heads.4 = bf16[4,256,128]{2,1,0:T(8,128)(2,1)} custom-call(bf16[4,256,128]{2,1,0:T(8,128)(2,1)} %get-tuple-element.56.src), custom_call_target="tpu_custom_call" | custom-call | tf_op jit(solution)/shard_map/swap_heads/pallas_call | solution.py:484
  249.2 56.0 %attend_back.1 = (bf16[1024,128]{1,0:T(8,128)(2,1)}, bf16[8192,256]{1,0:T(8,128)(2,1)}) custom-call(s32[2,6]{1,0:T(2,128)} %pad_add_fusion.bounds, bf16[1024,128]{1,0:T(8,128)(2,1)} %bitcast.42, bf16[8192,256]{1,0:T(8,128)(2,1)} %bitcast.37, bf16[1024,128]{1,0:T(8,128)(2,1)} %bitcast.43, f32[128,1024]{1,0:T(8,128)} %get-tuple-element.57.out_t, ...), custom_call_target="tpu_custom_call" | custom-call | tf_op jit(solution)/shard_map/attend_back/pallas_call | solution.py:750
  305.2 2.2 copy-done
  307.4 82.5 %collect_rows.1 = bf16[1024,256]{1,0:T(8,128)(2,1)S(1)} custom-call(bf16[8,1024,256]{2,1,0:T(8,128)(2,1)S(1)} %bitcast.35), custom_call_target="tpu_custom_call" | custom-call | tf_op jit(solution)/shard_map/collect_rows/pallas_call | solution.py:558
  390.0 1.0 pad_maximum_fusion.1
  391.0 11.4 %swap_heads.5.d_projected = bf16[4,256,384]{2,1,0:T(8,128)(2,1)} custom-call(bf16[4,256,384]{2,1,0:T(8,128)(2,1)} %bitcast.39), custom_call_target="tpu_custom_call" | custom-call | tf_op jit(solution)/shard_map/swap_heads/pallas_call | solution.py:484
  402.3 0.0 copy-start.4
  402.3 16.8 %ending.1 = (bf16[8,4,1168,128]{3,2,1,0:T(8,128)(2,1)}, bf16[3152,128]{1,0:T(8,128)(2,1)}) custom-call(s32[2,6]{1,0:T(2,128)} %pad_add_fusion.bounds, bf16[8,4,1168,128]{3,2,1,0:T(8,128)(2,1)} %get-tuple-element.55.grads_in, bf16[4,256,384]{2,1,0:T(8,128)(2,1)} %swap_heads.5.d_projected, ...), custom_call_target="tpu_custom_call", output_to_operand_aliasing={{0}: (1, {})} | custom-call | tf_op jit(solution)/shard_map/ending/pallas_call | solution.py:1339
  419.1 0.0 copy-done.4
  419.1 2.5 pad_maximum_fusion
  421.6 2.1 reshape.86
  423.7 1.4 pad.20
  425.1 94.4 %reduce_gradients.1 = (f32[1168,128]{1,0:T(8,128)}, f32[240,128]{1,0:T(8,128)}, f32[8,128]{1,0:T(8,128)}, bf16[4,240,128]{2,1,0:T(8,128)(2,1)}) custom-call(bf16[8,4,1168,128]{3,2,1,0:T(8,128)(2,1)} %get-tuple-element.74.refs_0_, bf16[8,4,240,128]{3,2,1,0:T(8,128)(2,1)} %bitcast.38, f32[8,128]{1,0:T(8,128)} %get-tuple-element.77.refs_2_), custom_call_target="tpu_custom_call" | custom-call | tf_op jit(solution)/shard_map/reduce_gradients/pallas_call | solution.py:345
  519.5 0.0 copy-start.6
  519.5 0.0 copy-start.7
  519.5 1.4 slice.29
  521.6 1.2 slice_bitcast_fusion
  522.8 0.0 copy-done.3
  522.9 2.5 fusion.5
  525.4 0.0 copy-done.7
  525.4 1.6 fusion.7
  (19 shorter events, 0.1 us)
Async XLA Ops:
  0.6 5.1 copy-start.1
  0.7 5.8 %copy-start.5 = (bf16[512,704]{0,1:T(8,128)(2,1)S(1)}, bf16[512,704]{0,1:T(8,128)(2,1)}, u32[]{:S(2)}) copy-start(bf16[512,704]{0,1:T(8,128)(2,1)} %param.12) | copy-start | bytes 2162692
  3.6 4.0 copy-start.11
  5.0 2.6 copy-start.2
  305.2 2.2 copy-start
  307.4 82.5 %copy-start.10 = (bf16[1024,128]{1,0:T(8,128)(2,1)S(1)}, bf16[1024,128]{1,0:T(8,128)(2,1)}, u32[]{:S(2)}) copy-start(bf16[1024,128]{1,0:T(8,128)(2,1)} %get-tuple-element.59) | copy-start | bytes 786436
  402.3 16.8 %copy-start.4 = (bf16[4104,128]{1,0:T(8,128)(2,1)S(1)}, bf16[4104,128]{1,0:T(8,128)(2,1)}, u32[]{:S(2)}) copy-start(bf16[4104,128]{1,0:T(8,128)(2,1)} %get-tuple-element.75) | copy-start | bytes 3151876
  425.1 97.8 %copy-start.3 = (f32[116096]{0:T(1024)S(1)}, f32[116096]{0:T(1024)}, u32[]{:S(2)}) copy-start(f32[116096]{0:T(1024)} %param.21) | copy-start | bytes 1393156
  425.1 97.8 %copy-start.9 = (f32[116096]{0:T(1024)S(1)}, f32[116096]{0:T(1024)}, u32[]{:S(2)}) copy-start(f32[116096]{0:T(1024)} %param.22) | copy-start | bytes 1393156
  519.5 5.9 %copy-start.6 = (f32[148480]{0:T(1024)S(1)}, f32[148480]{0:T(1024)}, u32[]{:S(2)}) copy-start(f32[148480]{0:T(1024)} %param.19) | copy-start | bytes 1781764
  519.5 5.9 %copy-start.7 = (f32[148480]{0:T(1024)S(1)}, f32[148480]{0:T(1024)}, u32[]{:S(2)}) copy-start(f32[148480]{0:T(1024)} %param.20) | copy-start | bytes 1781764
  519.5 5.9 %copy-start.8 = (f32[1168,128]{1,0:T(8,128)S(1)}, f32[1168,128]{1,0:T(8,128)}, u32[]{:S(2)}) copy-start(f32[1168,128]{1,0:T(8,128)} %get-tuple-element.78) | copy-start | bytes 1794052
